TPU v7x, 512 devices: a whole 4x8x8 slice. The times are simulated.
512 devices in a mesh: dp: 8 (over y_hi, core), fsdp: 64 (over y_lo, x, z).
Axes of the slice: x: 4, y: 8 (y_hi: 4, y_lo: 2; y = y_hi * 2 + y_lo), z: 8, core: 2. Of those that a mesh axis runs over, the one named last changes fastest.
Arguments:
- residual: bfloat16 [131072, 3200], P(('dp', 'fsdp')), may hold values from -6 to 6
- heads_out: bfloat16 [131072, 2048], P(('dp', 'fsdp')), may hold values from -6 to 6
- out_weight: bfloat16 [2048, 3200], P(('dp', 'fsdp')), may hold values from -0.125 to 0.125
- out_bias: float32 [3200], replicated, may hold values from -3 to 3
- layer_scale: float32 [3200], replicated, may hold values from 0.3 to 3
Outputs:
- updated: bfloat16 [131072, 3200], P(('dp', 'fsdp'))
All inputs are finite; a program needn't handle non-finite values.
Results may differ from a plain program's by a relative error of at most 0.001.
Values may be sent and summed in bfloat16 or wider, within the bound.
No kernel may reach another device: no remote copies, remote signals or barrier semaphores. Data moves between devices by JAX's collectives and lax.ppermute only.
A program may use at most 128 MiB of HBM per device.

v0:
```python
import jax
import jax.numpy as jnp
from jax import lax
from jax.sharding import PartitionSpec as P


def body(residual, heads_out, out_weight, out_bias, layer_scale):
    whole_weight = lax.all_gather(out_weight, ("dp", "fsdp"), axis=0, tiled=True)
    projected = jnp.dot(heads_out, whole_weight, preferred_element_type=jnp.float32)
    branch = layer_scale * (projected + out_bias)
    return (residual.astype(jnp.float32) + branch).astype(jnp.bfloat16)


def solution(mesh):
    return jax.shard_map(
        body,
        mesh=mesh,
        in_specs=(
            P(("dp", "fsdp"), None),
            P(("dp", "fsdp"), None),
            P(("dp", "fsdp"), None),
            P(),
            P(),
        ),
        out_specs=P(("dp", "fsdp"), None),
        check_vma=False,
    )
```

profile of v0, /device:TPU:1, one launch (start us, length us, event | category | flops | bytes accessed | tf_op | source)
XLA Modules:
  0.0 1479.7 jit_solution(10323708084143913214)
XLA Ops:
  6.5 0.0 copy-start
  6.5 0.0 all-gather.3.cloned.1.call-start
  6.5 0.7 all-gather.3.cloned.1.call-update
  7.3 0.0 copy-start.1
  7.3 0.0 copy-start.2
  7.3 0.0 copy-start.3
  7.3 1435.4 %all-gather.3.cloned.1.call-done = bf16[512,4,3200]{2,1,0:T(4,128)(2,1)} async-done(((bf16[1,4,3200]{2,1,0:T(4,128)(2,1)}), bf16[512,4,3200]{2,1,0:T(4,128)(2,1)}) %all-gather.3.cloned.1.call-update) | async-done | bytes 13107216 | tf_op jit(solution)/shard_map/all_gather | solution.py:8
  1442.7 20.6 %reshape.3 = bf16[2048,3200]{1,0:T(8,128)(2,1)} reshape(bf16[512,4,3200]{2,1,0:T(4,128)(2,1)} %all-gather.3.cloned.1.call-done) | data formatting | bytes 26214400
  1463.3 0.0 copy-done
  1463.3 0.0 copy-done.1
  1463.3 0.0 copy-done.2
  1463.3 0.0 copy-done.3
  1463.3 9.6 fusion.2
Async XLA Ops:
  6.5 1456.8 %copy-start = (bf16[256,2048]{1,0:T(8,128)(2,1)S(1)}, bf16[256,2048]{1,0:T(8,128)(2,1)}, u32[]{:S(2)}) copy-start(bf16[256,2048]{1,0:T(8,128)(2,1)} %param.6) | copy-start | bytes 3145732
  6.5 1436.2 %all-gather.3.cloned.1.call-start = ((), (), s32[]{:S(2)}) async-start(), calls=%async_computation | async-start | bytes 13132800 | tf_op jit(solution)/shard_map/all_gather | solution.py:8
  7.3 1456.0 %copy-start.1 = (bf16[256,3200]{1,0:T(8,128)(2,1)S(1)}, bf16[256,3200]{1,0:T(8,128)(2,1)}, u32[]{:S(2)}) copy-start(bf16[256,3200]{1,0:T(8,128)(2,1)} %param.5) | copy-start | bytes 4915204
  7.3 1456.0 %copy-start.2 = (f32[3200]{0:T(1024)S(1)}, f32[3200]{0:T(1024)}, u32[]{:S(2)}) copy-start(f32[3200]{0:T(1024)} %param.8) | copy-start | bytes 38404
  7.3 1456.0 %copy-start.3 = (f32[3200]{0:T(1024)S(1)}, f32[3200]{0:T(1024)}, u32[]{:S(2)}) copy-start(f32[3200]{0:T(1024)} %param.9) | copy-start | bytes 38404
Sparse Core Ops, SparseCore 0:
  9.6 1433.0 all-gather.2
where the time goes:
time: 1480 us
  waiting for transfers between devices  1440 us (97%)
  local copies, waits for them, and re-layouts  20.6 us (1%)
    all_gather x1, waiting for transfers between devices, body(): lax.all_gather(out_weight, ('dp', 'fsdp'), axis=0, tiled=True)  1440 us
  transfers between devices with their start and end apart: 1, of which 1 were waited for; matrix products, arithmetic and copies ran while one was open for 0% of the time, Pallas kernels for 0%

commit v1 on v0

v1 whole, which is shorter than its diff:
```python
import jax
import jax.numpy as jnp
import numpy as np
from jax import lax
from jax.sharding import Mesh, PartitionSpec as P

D = 3200
WIDE = 1664
SKIP = D - WIDE
Y, CORES, X, Z = 8, 2, 4, 8
DEVICES = Y * CORES * X * Z
CLASSES = 8
ROWS = 4
DEPTH = DEVICES * ROWS // CLASSES


def index_of(core, x, y, z):
    y, x, z = y % Y, x % X, z % Z
    return (((y // 2 * CORES + core) * 2 + y % 2) * X + x) * Z + z


def places():
    for core in range(CORES):
        for x in range(X):
            for y in range(Y):
                for z in range(Z):
                    yield core, x, y, z


def class_of(x, y, z):
    return (2 * x + y + 3 * z) % CLASSES


def class_groups():
    groups = [[] for _ in range(CLASSES)]
    for core, x, y, z in places():
        groups[class_of(x, y, z)].append(index_of(core, x, y, z))
    return [sorted(g) for g in groups]


def shift(dx, dy, dz, dx1=None, dy1=None, dz1=None):
    if dx1 is None:
        dx1, dy1, dz1 = dx, dy, dz
    pairs = []
    for core, x, y, z in places():
        ex, ey, ez = (dx, dy, dz) if core == 0 else (dx1, dy1, dz1)
        pairs.append((index_of(core, x, y, z), index_of(core, x + ex, y + ey, z + ez)))
    return pairs


OTHER_CORE = [(index_of(c, x, y, z), index_of(1 - c, x, y, z)) for c, x, y, z in places()]
GROUPS = class_groups()
ORDER = np.array([d * ROWS + i for g in GROUPS for d in g for i in range(ROWS)])
MOVES = [
    (shift(0, 1, 1, 0, -1, -1), 4),
    (shift(0, 1, 0), -1),
    (shift(0, -1, 0), 1),
    (shift(0, 0, 1), -3),
    (shift(0, 0, -1), 3),
    (shift(1, 0, 0), -2),
    (shift(-1, 0, 0), 2),
]


def body(residual, heads_out, out_weight, out_bias, layer_scale):
    me = lax.axis_index("d")
    core = me // (2 * X * Z) % CORES
    z = me % Z
    x = me // Z % X
    y = me // (CORES * 2 * X * Z) * 2 + me // (X * Z) % 2
    mine = (2 * x + y + 3 * z) % CLASSES
    first = core * SKIP

    halves = jnp.stack([out_weight[:, :WIDE], out_weight[:, SKIP:]])
    cores = np.array([g // (2 * X * Z) % CORES for g in GROUPS[0]])
    for_each = halves[cores]
    block = lax.all_to_all(for_each, "d", 0, 0, axis_index_groups=GROUPS, tiled=True)
    block = block.reshape(DEPTH, WIDE)
    blocks = [block] + [lax.ppermute(block, "d", pairs) for pairs, _ in MOVES]

    pick = (lax.broadcasted_iota(jnp.int32, (2048, 2048), 0) == ORDER.astype(np.int32)[None, :]).astype(jnp.bfloat16)
    own_heads = jnp.dot(heads_out, pick, preferred_element_type=jnp.float32).astype(jnp.bfloat16)
    heads = jnp.stack([own_heads, lax.ppermute(own_heads, "d", OTHER_CORE)])
    own_part = lax.dynamic_slice_in_dim(residual, first, WIDE, 1)
    other_part = lax.dynamic_slice_in_dim(residual, SKIP - first, WIDE, 1)
    came = lax.ppermute(other_part, "d", OTHER_CORE)
    stream = jnp.stack([own_part, came])
    scale = lax.dynamic_slice_in_dim(layer_scale, first, WIDE, 0)
    bias = lax.dynamic_slice_in_dim(out_bias, first, WIDE, 0)

    total = 0.0
    for part, more in zip(blocks, [0] + [m for _, m in MOVES]):
        at = (mine + more) % CLASSES * DEPTH
        cols = lax.dynamic_slice_in_dim(heads, at, DEPTH, 2)
        total = total + jnp.dot(cols.reshape(512, DEPTH), part, preferred_element_type=jnp.float32)
    total = total.reshape(2, 256, WIDE)
    updated = (stream.astype(jnp.float32) + scale * (total + bias)).astype(jnp.bfloat16)
    own, other = updated[0], lax.ppermute(updated[1], "d", OTHER_CORE)
    low = jnp.where(core == 0, own[:, :SKIP], other[:, :SKIP])
    mid = jnp.where(core == 0, own[:, SKIP:], own[:, : WIDE - SKIP])
    high = jnp.where(core == 0, other[:, WIDE - SKIP :], own[:, WIDE - SKIP :])
    return jnp.concatenate([low, mid, high], axis=1)


def solution(mesh):
    line = Mesh(mesh.devices.reshape(-1), ("d",))
    return jax.shard_map(
        body,
        mesh=line,
        in_specs=(P("d", None), P("d", None), P("d", None), P(), P()),
        out_specs=P("d", None),
        check_vma=False,
    )
```

time: 1480 us -> 127 us (0.09)
  waiting for transfers between devices: 1440 us -> 47.2 us
  starting transfers between devices: 0.01 us -> 50.4 us
    all_gather x1 -> x0, waiting for transfers between devices: 1440 us -> none  [body(): lax.all_gather(out_weight, ('dp', 'fsdp'), axis=0, tiled=True)]
    ppermute x0 -> x10, starting transfers between devices: none -> 31 us  [the longest x7 21.8 us: body(): blocks = [block] + [lax.ppermute(block, 'd', pairs) for pairs, _ in MOVES]]
    ppermute x0 -> x10, waiting for transfers between devices: none -> 24.4 us  [the longest x7 22.3 us: body(): blocks = [block] + [lax.ppermute(block, 'd', pairs) for pairs, _ in MOVES]]
    all_to_all x0 -> x1, waiting for transfers between devices: none -> 22.8 us  [body(): lax.all_to_all(for_each, 'd', 0, 0, axis_index_groups=GROUPS, tiled=True)]
    unnamed x9 -> x12, local copies, waits for them, and re-layouts: 20.6 us -> 0.03 us
    all_to_all x0 -> x1, starting transfers between devices: none -> 19.5 us  [body(): lax.all_to_all(for_each, 'd', 0, 0, axis_index_groups=GROUPS, tiled=True)]
  transfers between devices with their start and end apart: 1 -> 11, of which waited for: 1 -> 5; matrix products, arithmetic and copies ran while one was open for 0% -> 15% of each run, Pallas kernels for 0% -> 0%
where the time goes in v1:
time: 127 us; the launch traced here: 126 us
  starting transfers between devices  50.4 us (40%)
  waiting for transfers between devices  47.2 us (37%)
  matrix products  14 us (11%)
  local copies, waits for them, and re-layouts  8.34 us (7%)
  other arithmetic  5.47 us (4%)
    all_to_all x1, waiting for transfers between devices, body(): lax.all_to_all(for_each, 'd', 0, 0, axis_index_groups=GROUPS, tiled=True)  22.8 us
    ppermute x7, waiting for transfers between devices, body(): blocks = [block] + [lax.ppermute(block, 'd', pairs) for pairs, _ in MOVES]  22.3 us
    ppermute x7, starting transfers between devices, body(): blocks = [block] + [lax.ppermute(block, 'd', pairs) for pairs, _ in MOVES]  21.8 us
    all_to_all x1, starting transfers between devices, body(): lax.all_to_all(for_each, 'd', 0, 0, axis_index_groups=GROUPS, tiled=True)  19.5 us
    dot_general x8, matrix products, body(): jnp.dot(cols.reshape(512, DEPTH), part, preferred_element_type=jnp.float32)  10.8 us
    ppermute x1, starting transfers between devices, body(): own, other = (updated[0], lax.ppermute(updated[1], 'd', OTHER_CORE))  3.81 us
    dot_general x1, matrix products, body(): jnp.dot(heads_out, pick, preferred_element_type=jnp.float32)  3.17 us
    ppermute x1, starting transfers between devices, body(): came = lax.ppermute(other_part, 'd', OTHER_CORE)  2.93 us
  transfers between devices with their start and end apart: 11, of which 5 were waited for; matrix products, arithmetic and copies ran while one was open for 15% of the time, Pallas kernels for 0%

profile of v1, /device:TPU:1, one launch (start us, length us, event | category | flops | bytes accessed | tf_op | source)
XLA Modules:
  0.0 125.9 jit_solution(14669891975942934135)
XLA Ops:
  0.0 0.0 copy-start
  0.0 0.0 copy-start.5
  0.0 0.8 slice_bitcast_fusion.3
  0.8 0.7 pad_clamp_fusion
  1.5 2.1 %gather_fusion = bf16[64,4,1664]{2,1,0:T(4,128)(2,1)} fusion(bf16[2,4,1664]{2,1,0:T(4,128)(2,1)S(1)} %pad_maximum_fusion.1, s32[1024]{0:T(1024)S(1)} %pad_clamp_fusion), kind=kCustom, calls=%fused_computation | custom fusion | bytes 1704192 | tf_op jit(solution)/shard_map/gather | solution.py:76
  3.7 19.5 %all-to-all-start = ((bf16[64,4,1664]{2,1,0:T(4,128)(2,1)}), bf16[64,4,1664]{2,1,0:T(4,128)(2,1)}, u32[]{:S(2)}, u32[]{:S(2)}) async-start(bf16[64,4,1664]{2,1,0:T(4,128)(2,1)} %gather_fusion), calls=%async_computation | async-start | bytes 1703936 | tf_op jit(solution)/shard_map/all_to_all | solution.py:77
  23.1 0.0 copy-done
  23.1 0.0 copy-done.5
  23.2 3.2 %fusion.2 = bf16[2048,256]{0,1:T(8,128)(2,1)S(1)} fusion(bf16[256,2048]{1,0:T(8,128)(2,1)S(1)} %copy-done, s32[2048]{0:T(1024)S(1)} %copy-done.5), kind=kOutput, calls=%fused_computation.22 | convolution fusion | flops 2152202240 | bytes 2105344 | tf_op jit(solution)/shard_map/dot_general | solution.py:82
  26.3 0.0 copy-start.3
  26.3 0.0 copy-start.4
  26.4 2.4 %collective-permute-start.1 = (bf16[256,2048]{1,0:T(8,128)(2,1)S(1)}, bf16[256,2048]{1,0:T(8,128)(2,1)S(1)}, u32[]{:S(2)}, u32[]{:S(2)}) collective-permute-start(bf16[256,2048]{1,0:T(8,128)(2,1)S(1)} %bitcast.42), channel_id=1, source_target_pairs={{0,64},{1,65},{2,66},{3,67},{4,68},{5,69},{6,70},{7,71},{32,96},{3... | collective-permute-start | bytes 3145736 | tf_op jit(solution)/shard_map/ppermute | solution.py:83
  28.8 22.8 %all-to-all-done = bf16[64,4,1664]{2,1,0:T(4,128)(2,1)} async-done(((bf16[64,4,1664]{2,1,0:T(4,128)(2,1)}), bf16[64,4,1664]{2,1,0:T(4,128)(2,1)}, u32[]{:S(2)}, u32[]{:S(2)}) %all-to-all-start) | async-done | bytes 852000 | tf_op jit(solution)/shard_map/all_to_all | solution.py:77
  51.6 2.3 %reshape.33 = bf16[256,1664]{1,0:T(8,128)(2,1)} reshape(bf16[64,4,1664]{2,1,0:T(4,128)(2,1)} %all-to-all-done) | data formatting | bytes 1703936 | tf_op jit(solution)/shard_map/reshape | solution.py:78
  53.9 1.9 %collective-permute-start.2 = (bf16[256,1664]{1,0:T(8,128)(2,1)}, bf16[256,1664]{1,0:T(8,128)(2,1)}, u32[]{:S(2)}, u32[]{:S(2)}) collective-permute-start(bf16[256,1664]{1,0:T(8,128)(2,1)} %reshape.33), channel_id=1, source_target_pairs={{0,33},{1,34},{2,35},{3,36},{4,37},{5,38},{6,39},{7,32},{32,129},{... | collective-permute-start | bytes 2555912 | tf_op jit(solution)/shard_map/ppermute | solution.py:79
  55.8 2.7 %dynamic-slice_bitcast_fusion = (bf16[1,256,1664]{2,1,0:T(8,128)(2,1)}, bf16[256,1664]{1,0:T(8,128)(2,1)}) fusion(bf16[256,3200]{1,0:T(8,128)(2,1)} %param.8, s32[]{:T(128)S(6)} %select_n.126, s32[]{:T(128)S(6)} %select_n.127), kind=kLoop, calls=%fused_computation.26 | loop fusion | bytes 3407880 | tf_op jit(solution)/shard_map/stack | solution.py:87
  58.6 2.9 %collective-permute-start = (bf16[256,1664]{1,0:T(8,128)(2,1)}, bf16[256,1664]{1,0:T(8,128)(2,1)}, u32[]{:S(2)}, u32[]{:S(2)}) collective-permute-start(bf16[256,1664]{1,0:T(8,128)(2,1)} %get-tuple-element.18), channel_id=1, source_target_pairs={{0,64},{1,65},{2,66},{3,67},{4,68},{5,69},{6,70},{7,71},{32,96},{3... | collective-permute-start | bytes 2555912 | tf_op jit(solution)/shard_map/ppermute | solution.py:86
  61.7 0.0 copy-done.3
  61.7 0.1 dynamic_slice.38
  61.8 0.0 copy-done.4
  61.8 0.1 dynamic_slice.47
  61.9 0.0 copy-start.2
  61.9 3.3 %collective-permute-start.3 = (bf16[256,1664]{1,0:T(8,128)(2,1)}, bf16[256,1664]{1,0:T(8,128)(2,1)S(1)}, u32[]{:S(2)}, u32[]{:S(2)}) collective-permute-start(bf16[256,1664]{1,0:T(8,128)(2,1)} %reshape.33), channel_id=1, source_target_pairs={{0,32},{1,33},{2,34},{3,35},{4,36},{5,37},{6,38},{7,39},{32,128},{... | collective-permute-start | bytes 2555912 | tf_op jit(solution)/shard_map/ppermute | solution.py:79
  65.2 0.0 collective-permute-done.1
  65.3 0.1 fusion.10
  65.3 0.2 fusion.5
  65.6 0.0 copy-done.2
  65.6 3.3 %collective-permute-start.4 = (bf16[256,1664]{1,0:T(8,128)(2,1)S(1)}, bf16[256,1664]{1,0:T(8,128)(2,1)S(1)}, u32[]{:S(2)}, u32[]{:S(2)}) collective-permute-start(bf16[256,1664]{1,0:T(8,128)(2,1)S(1)} %copy-done.2), channel_id=1, source_target_pairs={{0,416},{1,417},{2,418},{3,419},{4,420},{5,421},{6,422},{7,423},{3... | collective-permute-start | bytes 2555912 | tf_op jit(solution)/shard_map/ppermute | solution.py:79
  68.9 3.0 %collective-permute-start.5 = (bf16[256,1664]{1,0:T(8,128)(2,1)S(1)}, bf16[256,1664]{1,0:T(8,128)(2,1)S(1)}, u32[]{:S(2)}, u32[]{:S(2)}) collective-permute-start(bf16[256,1664]{1,0:T(8,128)(2,1)S(1)} %copy-done.2), channel_id=1, source_target_pairs={{0,1},{1,2},{2,3},{3,4},{4,5},{5,6},{6,7},{7,0},{32,33},{33,34},{3... | collective-permute-start | bytes 2555912 | tf_op jit(solution)/shard_map/ppermute | solution.py:79
  72.0 0.6 fusion.11
  72.6 0.0 collective-permute-done.2
  72.6 3.5 %collective-permute-start.6 = (bf16[256,1664]{1,0:T(8,128)(2,1)S(1)}, bf16[256,1664]{1,0:T(8,128)(2,1)S(1)}, u32[]{:S(2)}, u32[]{:S(2)}) collective-permute-start(bf16[256,1664]{1,0:T(8,128)(2,1)S(1)} %copy-done.2), channel_id=1, source_target_pairs={{0,7},{1,0},{2,1},{3,2},{4,3},{5,4},{6,5},{7,6},{32,39},{33,32},{3... | collective-permute-start | bytes 2555912 | tf_op jit(solution)/shard_map/ppermute | solution.py:79
  76.2 1.8 %fusion.12 = f32[512,1664]{1,0:T(8,128)S(1)} fusion(bf16[512,256]{1,0:T(8,128)(2,1)S(1)} %bitcast.53, bf16[256,1664]{1,0:T(8,128)(2,1)} %collective-permute-done.2), kind=kOutput, calls=%fused_computation.44 | convolution fusion | flops 436207616 | bytes 4521984 | tf_op jit(solution)/shard_map/dot_general | solution.py:95
  77.9 8.5 %collective-permute-done.3 = bf16[256,1664]{1,0:T(8,128)(2,1)S(1)} collective-permute-done((bf16[256,1664]{1,0:T(8,128)(2,1)}, bf16[256,1664]{1,0:T(8,128)(2,1)S(1)}, u32[]{:S(2)}, u32[]{:S(2)}) %collective-permute-start.3) | collective-permute-done | bytes 852000 | tf_op jit(solution)/shard_map/ppermute | solution.py:79
  86.4 3.5 %collective-permute-start.7 = (bf16[256,1664]{1,0:T(8,128)(2,1)S(1)}, bf16[256,1664]{1,0:T(8,128)(2,1)S(1)}, u32[]{:S(2)}, u32[]{:S(2)}) collective-permute-start(bf16[256,1664]{1,0:T(8,128)(2,1)S(1)} %copy-done.2), channel_id=1, source_target_pairs={{0,8},{1,9},{2,10},{3,11},{4,12},{5,13},{6,14},{7,15},{32,40},{33,... | collective-permute-start | bytes 2555912 | tf_op jit(solution)/shard_map/ppermute | solution.py:79
  89.9 0.6 fusion.13
  90.5 0.0 collective-permute-done.4
  90.5 3.2 %collective-permute-start.8 = (bf16[256,1664]{1,0:T(8,128)(2,1)S(1)}, bf16[256,1664]{1,0:T(8,128)(2,1)S(1)}, u32[]{:S(2)}, u32[]{:S(2)}) collective-permute-start(bf16[256,1664]{1,0:T(8,128)(2,1)S(1)} %copy-done.2), channel_id=1, source_target_pairs={{0,24},{1,25},{2,26},{3,27},{4,28},{5,29},{6,30},{7,31},{32,56},{3... | collective-permute-start | bytes 2555912 | tf_op jit(solution)/shard_map/ppermute | solution.py:79
  93.7 0.6 fusion.14
  94.4 0.0 collective-permute-done.5
  94.4 0.6 fusion.15
  95.0 0.0 collective-permute-done.6
  95.1 0.6 fusion.16
  95.7 11.7 %collective-permute-done.7 = bf16[256,1664]{1,0:T(8,128)(2,1)S(1)} collective-permute-done((bf16[256,1664]{1,0:T(8,128)(2,1)S(1)}, bf16[256,1664]{1,0:T(8,128)(2,1)S(1)}, u32[]{:S(2)}, u32[]{:S(2)}) %collective-permute-start.7) | collective-permute-done | bytes 852000 | tf_op jit(solution)/shard_map/ppermute | solution.py:79
  107.4 2.4 %fusion.17 = f32[512,1664]{1,0:T(8,128)} fusion(bf16[512,256]{1,0:T(8,128)(2,1)S(1)} %bitcast.48, bf16[256,1664]{1,0:T(8,128)(2,1)S(1)} %collective-permute-done.7), kind=kOutput, calls=%fused_computation.49 | convolution fusion | flops 436207616 | bytes 4521984 | tf_op jit(solution)/shard_map/dot_general | solution.py:95
  109.8 2.1 %collective-permute-done.8 = bf16[256,1664]{1,0:T(8,128)(2,1)S(1)} collective-permute-done((bf16[256,1664]{1,0:T(8,128)(2,1)S(1)}, bf16[256,1664]{1,0:T(8,128)(2,1)S(1)}, u32[]{:S(2)}, u32[]{:S(2)}) %collective-permute-start.8) | collective-permute-done | bytes 852000 | tf_op jit(solution)/shard_map/ppermute | solution.py:79
  111.9 0.0 copy-start.1
  111.9 3.4 %add_add_fusion = f32[512,1664]{1,0:T(8,128)S(1)} fusion(f32[512,1664]{1,0:T(8,128)} %fusion.17, f32[512,1664]{1,0:T(8,128)S(1)} %fusion.16, f32[512,1664]{1,0:T(8,128)S(1)} %fusion.15, f32[512,1664]{1,0:T(8,128)S(1)} %fusion.14, f32[512,1664]{1,0:T(8,128)S(1)} %fusion.13, f32[512,1664]{1,0:T(8,128)S(1)} %fusion.11, f32[512,1664]{1,0:T(8,128)S(1)} %fusion.12, ...), kind=kOutput, calls=%fused_computation.21 | convolution fusion | flops 442171392 | bytes 28377088 | tf_op jit(solution)/shard_map/dot_general | solution.py:95
  115.3 0.0 collective-permute-done
  115.4 0.0 copy-done.1
  115.4 1.7 %add_convert_fusion = bf16[2,256,1664]{2,1,0:T(8,128)(2,1)S(1)} fusion(f32[2,256,1664]{2,1,0:T(8,128)S(1)} %bitcast.41, bf16[1,256,1664]{2,1,0:T(8,128)(2,1)} %bitcast.1, bf16[1,256,1664]{2,1,0:T(8,128)(2,1)S(1)} %copy-done.1, f32[1664]{0:T(1024)S(1)} %dynamic_slice.47, f32[1664]{0:T(1024)S(1)} %dynamic_slice.38), kind=kLoop, calls=%fused_computation.20 | loop fusion | flops 5111808 | bytes 6829056 | tf_op jit(solution)/shard_map/convert_element_type | solution.py:97
  117.0 0.1 slice_bitcast_fusion
  117.2 3.8 %collective-permute-start.9 = (bf16[256,1664]{1,0:T(8,128)(2,1)S(1)}, bf16[256,1664]{1,0:T(8,128)(2,1)}, u32[]{:S(2)}, u32[]{:S(2)}) collective-permute-start(bf16[256,1664]{1,0:T(8,128)(2,1)S(1)} %get-tuple-element.15), channel_id=1, source_target_pairs={{0,64},{1,65},{2,66},{3,67},{4,68},{5,69},{6,70},{7,71},{32,96},{3... | collective-permute-start | bytes 2555912 | tf_op jit(solution)/shard_map/ppermute | solution.py:98
  121.0 2.1 %collective-permute-done.9 = bf16[256,1664]{1,0:T(8,128)(2,1)} collective-permute-done((bf16[256,1664]{1,0:T(8,128)(2,1)S(1)}, bf16[256,1664]{1,0:T(8,128)(2,1)}, u32[]{:S(2)}, u32[]{:S(2)}) %collective-permute-start.9) | collective-permute-done | bytes 852000 | tf_op jit(solution)/shard_map/ppermute | solution.py:98
  123.1 1.5 %slice_select_fusion.1 = (bf16[256,1536]{1,0:T(8,128)(2,1)S(1)}, bf16[256,1536]{1,0:T(8,128)(2,1)S(1)}) fusion(bf16[256,1664]{1,0:T(8,128)(2,1)} %collective-permute-done.9, bf16[256,1664]{1,0:T(8,128)(2,1)S(1)} %get-tuple-element.16, pred[]{:T(512)S(6)} %eq.29), kind=kLoop, calls=%fused_computation.28 | loop fusion | flops 786432 | bytes 4718593 | tf_op jit(solution)/shard_map/jit(_where)/select_n | solution.py:99
  124.6 1.3 %pad_maximum_fusion = bf16[256,3200]{1,0:T(8,128)(2,1)} fusion(bf16[256,1536]{1,0:T(8,128)(2,1)S(1)} %get-tuple-element.14, bf16[256,128]{1,0:T(8,128)(2,1)S(1)} %slice_select_fusion.2, bf16[256,1536]{1,0:T(8,128)(2,1)S(1)} %get-tuple-element.13), kind=kLoop, calls=%fused_computation.23 | loop fusion | flops 4915200 | bytes 3276800 | tf_op jit(solution)/shard_map/concatenate | solution.py:102
  (2 shorter events, 0.0 us)
Async XLA Ops:
  0.0 23.1 %copy-start = (bf16[256,2048]{1,0:T(8,128)(2,1)S(1)}, bf16[256,2048]{1,0:T(8,128)(2,1)}, u32[]{:S(2)}) copy-start(bf16[256,2048]{1,0:T(8,128)(2,1)} %param.9) | copy-start | bytes 3145732
  0.0 23.1 %copy-start.5 = (s32[2048]{0:T(1024)S(1)}, s32[2048]{0:T(1024)}, u32[]{:S(2)}) copy-start(s32[2048]{0:T(1024)} %constant.151) | copy-start | bytes 24580
  3.7 47.9 %all-to-all-start = ((bf16[64,4,1664]{2,1,0:T(4,128)(2,1)}), bf16[64,4,1664]{2,1,0:T(4,128)(2,1)}, u32[]{:S(2)}, u32[]{:S(2)}) async-start(bf16[64,4,1664]{2,1,0:T(4,128)(2,1)} %gather_fusion), calls=%async_computation | async-start | bytes 1703936 | tf_op jit(solution)/shard_map/all_to_all | solution.py:77
  26.3 35.4 %copy-start.3 = (f32[3200]{0:T(1024)S(1)}, f32[3200]{0:T(1024)}, u32[]{:S(2)}) copy-start(f32[3200]{0:T(1024)} %param.12) | copy-start | bytes 38404
  26.3 35.5 %copy-start.4 = (f32[3200]{0:T(1024)S(1)}, f32[3200]{0:T(1024)}, u32[]{:S(2)}) copy-start(f32[3200]{0:T(1024)} %param.11) | copy-start | bytes 38404
  26.4 38.9 %collective-permute-start.1 = (bf16[256,2048]{1,0:T(8,128)(2,1)S(1)}, bf16[256,2048]{1,0:T(8,128)(2,1)S(1)}, u32[]{:S(2)}, u32[]{:S(2)}) collective-permute-start(bf16[256,2048]{1,0:T(8,128)(2,1)S(1)} %bitcast.42), channel_id=1, source_target_pairs={{0,64},{1,65},{2,66},{3,67},{4,68},{5,69},{6,70},{7,71},{32,96},{3... | collective-permute-start | bytes 3145736 | tf_op jit(solution)/shard_map/ppermute | solution.py:83
  53.9 18.7 %collective-permute-start.2 = (bf16[256,1664]{1,0:T(8,128)(2,1)}, bf16[256,1664]{1,0:T(8,128)(2,1)}, u32[]{:S(2)}, u32[]{:S(2)}) collective-permute-start(bf16[256,1664]{1,0:T(8,128)(2,1)} %reshape.33), channel_id=1, source_target_pairs={{0,33},{1,34},{2,35},{3,36},{4,37},{5,38},{6,39},{7,32},{32,129},{... | collective-permute-start | bytes 2555912 | tf_op jit(solution)/shard_map/ppermute | solution.py:79
  58.6 56.8 %collective-permute-start = (bf16[256,1664]{1,0:T(8,128)(2,1)}, bf16[256,1664]{1,0:T(8,128)(2,1)}, u32[]{:S(2)}, u32[]{:S(2)}) collective-permute-start(bf16[256,1664]{1,0:T(8,128)(2,1)} %get-tuple-element.18), channel_id=1, source_target_pairs={{0,64},{1,65},{2,66},{3,67},{4,68},{5,69},{6,70},{7,71},{32,96},{3... | collective-permute-start | bytes 2555912 | tf_op jit(solution)/shard_map/ppermute | solution.py:86
  61.9 3.7 %copy-start.2 = (bf16[256,1664]{1,0:T(8,128)(2,1)S(1)}, bf16[256,1664]{1,0:T(8,128)(2,1)}, u32[]{:S(2)}) copy-start(bf16[256,1664]{1,0:T(8,128)(2,1)} %reshape.33) | copy-start | bytes 2555908
  61.9 24.5 %collective-permute-start.3 = (bf16[256,1664]{1,0:T(8,128)(2,1)}, bf16[256,1664]{1,0:T(8,128)(2,1)S(1)}, u32[]{:S(2)}, u32[]{:S(2)}) collective-permute-start(bf16[256,1664]{1,0:T(8,128)(2,1)} %reshape.33), channel_id=1, source_target_pairs={{0,32},{1,33},{2,34},{3,35},{4,36},{5,37},{6,38},{7,39},{32,128},{... | collective-permute-start | bytes 2555912 | tf_op jit(solution)/shard_map/ppermute | solution.py:79
  65.6 25.0 %collective-permute-start.4 = (bf16[256,1664]{1,0:T(8,128)(2,1)S(1)}, bf16[256,1664]{1,0:T(8,128)(2,1)S(1)}, u32[]{:S(2)}, u32[]{:S(2)}) collective-permute-start(bf16[256,1664]{1,0:T(8,128)(2,1)S(1)} %copy-done.2), channel_id=1, source_target_pairs={{0,416},{1,417},{2,418},{3,419},{4,420},{5,421},{6,422},{7,423},{3... | collective-permute-start | bytes 2555912 | tf_op jit(solution)/shard_map/ppermute | solution.py:79
  68.9 25.5 %collective-permute-start.5 = (bf16[256,1664]{1,0:T(8,128)(2,1)S(1)}, bf16[256,1664]{1,0:T(8,128)(2,1)S(1)}, u32[]{:S(2)}, u32[]{:S(2)}) collective-permute-start(bf16[256,1664]{1,0:T(8,128)(2,1)S(1)} %copy-done.2), channel_id=1, source_target_pairs={{0,1},{1,2},{2,3},{3,4},{4,5},{5,6},{6,7},{7,0},{32,33},{33,34},{3... | collective-permute-start | bytes 2555912 | tf_op jit(solution)/shard_map/ppermute | solution.py:79
  72.6 22.4 %collective-permute-start.6 = (bf16[256,1664]{1,0:T(8,128)(2,1)S(1)}, bf16[256,1664]{1,0:T(8,128)(2,1)S(1)}, u32[]{:S(2)}, u32[]{:S(2)}) collective-permute-start(bf16[256,1664]{1,0:T(8,128)(2,1)S(1)} %copy-done.2), channel_id=1, source_target_pairs={{0,7},{1,0},{2,1},{3,2},{4,3},{5,4},{6,5},{7,6},{32,39},{33,32},{3... | collective-permute-start | bytes 2555912 | tf_op jit(solution)/shard_map/ppermute | solution.py:79
  86.4 21.0 %collective-permute-start.7 = (bf16[256,1664]{1,0:T(8,128)(2,1)S(1)}, bf16[256,1664]{1,0:T(8,128)(2,1)S(1)}, u32[]{:S(2)}, u32[]{:S(2)}) collective-permute-start(bf16[256,1664]{1,0:T(8,128)(2,1)S(1)} %copy-done.2), channel_id=1, source_target_pairs={{0,8},{1,9},{2,10},{3,11},{4,12},{5,13},{6,14},{7,15},{32,40},{33,... | collective-permute-start | bytes 2555912 | tf_op jit(solution)/shard_map/ppermute | solution.py:79
  90.5 21.4 %collective-permute-start.8 = (bf16[256,1664]{1,0:T(8,128)(2,1)S(1)}, bf16[256,1664]{1,0:T(8,128)(2,1)S(1)}, u32[]{:S(2)}, u32[]{:S(2)}) collective-permute-start(bf16[256,1664]{1,0:T(8,128)(2,1)S(1)} %copy-done.2), channel_id=1, source_target_pairs={{0,24},{1,25},{2,26},{3,27},{4,28},{5,29},{6,30},{7,31},{32,56},{3... | collective-permute-start | bytes 2555912 | tf_op jit(solution)/shard_map/ppermute | solution.py:79
  111.9 3.5 %copy-start.1 = (bf16[1,256,1664]{2,1,0:T(8,128)(2,1)S(1)}, bf16[1,256,1664]{2,1,0:T(8,128)(2,1)}, u32[]{:S(2)}) copy-start(bf16[1,256,1664]{2,1,0:T(8,128)(2,1)} %get-tuple-element.17) | copy-start | bytes 2555908
  117.2 5.9 %collective-permute-start.9 = (bf16[256,1664]{1,0:T(8,128)(2,1)S(1)}, bf16[256,1664]{1,0:T(8,128)(2,1)}, u32[]{:S(2)}, u32[]{:S(2)}) collective-permute-start(bf16[256,1664]{1,0:T(8,128)(2,1)S(1)} %get-tuple-element.15), channel_id=1, source_target_pairs={{0,64},{1,65},{2,66},{3,67},{4,68},{5,69},{6,70},{7,71},{32,96},{3... | collective-permute-start | bytes 2555912 | tf_op jit(solution)/shard_map/ppermute | solution.py:98

commit v2 on v1

v2 whole, which is shorter than its diff:
```python
import jax
import jax.numpy as jnp
import numpy as np
from jax import lax
from jax.experimental import pallas as pl
from jax.experimental.pallas import tpu as pltpu
from jax.sharding import Mesh, PartitionSpec as P

D = 3200
INNER = 2048
TOK = 256
WIDE = 1664
SKIP = D - WIDE
Y, CORES, X, Z = 8, 2, 4, 8
CLASSES = 8
ROWS = 4
DEPTH = INNER // CLASSES
MIB = 1 << 20


def index_of(core, x, y, z):
    y, x, z = y % Y, x % X, z % Z
    return (((y // 2 * CORES + core) * 2 + y % 2) * X + x) * Z + z


def places():
    for core in range(CORES):
        for y in range(Y):
            for x in range(X):
                for z in range(Z):
                    yield core, x, y, z


def class_of(x, y, z):
    return (2 * x + y + 3 * z) % CLASSES


def class_chips():
    chips = [[] for _ in range(CLASSES)]
    for core, x, y, z in places():
        if core == 0:
            chips[class_of(x, y, z)].append((x, y, z))
    return chips


def moves(step, step1=None):
    pairs = []
    for core, x, y, z in places():
        ex, ey, ez = step1 if core and step1 else step
        pairs.append((index_of(core, x, y, z), index_of(core, x + ex, y + ey, z + ez)))
    return pairs


CHIPS = class_chips()
GROUPS = [[index_of(core, *chip) for chip in chips] for core in range(CORES) for chips in CHIPS]
CHIP_PAIRS = [[index_of(0, x, y, z), index_of(1, x, y, z)] for core, x, y, z in places() if core == 0]
OTHER_CORE = [(index_of(c, x, y, z), index_of(1 - c, x, y, z)) for c, x, y, z in places()]
ORDER = np.array(
    [
        index_of(core, *chip) * ROWS + i
        for chips in CHIPS
        for chip in chips
        for core in range(CORES)
        for i in range(ROWS)
    ],
    np.int32,
)
STEPS = [
    ((1, 0, 0), None),
    ((-1, 0, 0), None),
    ((0, 1, 0), None),
    ((0, -1, 0), None),
    ((0, 0, 1), None),
    ((0, 0, -1), None),
    ((0, 1, 1), (0, -1, -1)),
]


def multiply(n, first_ref, *refs):
    pass


def early_kernel(n, rank_ref, heads_ref, *refs):
    total = None
    for k in range(n):
        part = jnp.dot(heads_ref[rank_ref[k]], refs[k][...], preferred_element_type=jnp.float32)
        total = part if total is None else total + part
    refs[n][...] = total


def late_kernel(n, rank_ref, heads_ref, early_ref, stream_ref, scale_ref, bias_ref, *refs):
    total = early_ref[...]
    for k in range(n):
        total = total + jnp.dot(heads_ref[rank_ref[k]], refs[k][...], preferred_element_type=jnp.float32)
    branch = scale_ref[...] * (total + bias_ref[...])
    refs[n][...] = (stream_ref[...].astype(jnp.float32) + branch).astype(jnp.bfloat16)


def join_kernel(core_ref, own_ref, other_ref, out_ref):
    @pl.when(core_ref[0] == 0)
    def _():
        out_ref[:, :WIDE] = own_ref[...]
        out_ref[:, WIDE:] = other_ref[:, WIDE - SKIP :]

    @pl.when(core_ref[0] == 1)
    def _():
        out_ref[:, :SKIP] = other_ref[:, :SKIP]
        out_ref[:, SKIP:] = own_ref[...]


def whole(shape):
    return pl.BlockSpec(shape, lambda i, *_: (0,) * len(shape))


PARTS = 4


def early(ranks, heads, blocks):
    n = len(blocks)
    rows = heads.shape[1]
    tile = rows // PARTS
    return pl.pallas_call(
        lambda *refs: early_kernel(n, *refs),
        grid_spec=pltpu.PrefetchScalarGridSpec(
            num_scalar_prefetch=1,
            grid=(PARTS,),
            in_specs=[pl.BlockSpec((CLASSES, tile, DEPTH), lambda i, *_: (0, i, 0))] + [whole((DEPTH, WIDE))] * n,
            out_specs=pl.BlockSpec((tile, WIDE), lambda i, *_: (i, 0)),
        ),
        out_shape=jax.ShapeDtypeStruct((rows, WIDE), jnp.float32),
        compiler_params=pltpu.CompilerParams(vmem_limit_bytes=32 * MIB),
        cost_estimate=pl.CostEstimate(flops=2 * rows * DEPTH * WIDE * n, bytes_accessed=8 * MIB, transcendentals=0),
    )(ranks, heads, *blocks)


def late(ranks, heads, total, stream, scale, bias, blocks):
    n = len(blocks)
    rows = heads.shape[1]
    tile = rows // 2
    return pl.pallas_call(
        lambda *refs: late_kernel(n, *refs),
        grid_spec=pltpu.PrefetchScalarGridSpec(
            num_scalar_prefetch=1,
            grid=(2,),
            in_specs=[
                pl.BlockSpec((CLASSES, tile, DEPTH), lambda i, *_: (0, i, 0)),
                pl.BlockSpec((tile, WIDE), lambda i, *_: (i, 0)),
                pl.BlockSpec((tile, WIDE), lambda i, *_: (i, 0)),
                whole((1, WIDE)),
                whole((1, WIDE)),
            ]
            + [whole((DEPTH, WIDE))] * n,
            out_specs=pl.BlockSpec((tile, WIDE), lambda i, *_: (i, 0)),
        ),
        out_shape=jax.ShapeDtypeStruct((rows, WIDE), jnp.bfloat16),
        compiler_params=pltpu.CompilerParams(vmem_limit_bytes=32 * MIB),
        cost_estimate=pl.CostEstimate(flops=2 * rows * DEPTH * WIDE * n, bytes_accessed=4 * MIB, transcendentals=0),
    )(ranks, heads, total, stream, scale, bias, *blocks)


def join(core, own, other):
    tile = TOK // 2
    return pl.pallas_call(
        join_kernel,
        grid_spec=pltpu.PrefetchScalarGridSpec(
            num_scalar_prefetch=1,
            grid=(2,),
            in_specs=[pl.BlockSpec((tile, WIDE), lambda i, *_: (i, 0))] * 2,
            out_specs=pl.BlockSpec((tile, D), lambda i, *_: (i, 0)),
        ),
        out_shape=jax.ShapeDtypeStruct((TOK, D), jnp.bfloat16),
        compiler_params=pltpu.CompilerParams(vmem_limit_bytes=16 * MIB),
    )(core.reshape(1), own, other)


def body(residual, heads_out, out_weight, out_bias, layer_scale):
    me = lax.axis_index("d")
    core = me // (2 * X * Z) % CORES
    z = me % Z
    x = me // Z % X
    y = me // (CORES * 2 * X * Z) * 2 + me // (X * Z) % 2
    mine = class_of(x, y, z)
    first = core * SKIP

    chip_rows = lax.all_gather(out_weight, "d", axis=0, axis_index_groups=CHIP_PAIRS)
    chip_rows = lax.dynamic_slice_in_dim(chip_rows, first, WIDE, 2).reshape(1, CORES * ROWS, WIDE)
    for_each = jnp.broadcast_to(chip_rows, (len(CHIPS[0]), CORES * ROWS, WIDE))
    block = lax.all_to_all(for_each, "d", 0, 0, axis_index_groups=GROUPS, tiled=True).reshape(DEPTH, WIDE)

    pick = (lax.broadcasted_iota(jnp.int32, (INNER, INNER), 0) == ORDER[None, :]).astype(jnp.bfloat16)
    own_heads = jnp.dot(heads_out, pick, preferred_element_type=jnp.float32).astype(jnp.bfloat16)
    own_heads = own_heads.reshape(TOK, CLASSES, DEPTH).transpose(1, 0, 2)
    other_heads = lax.ppermute(own_heads, "d", OTHER_CORE)
    own_stream = lax.dynamic_slice_in_dim(residual, first, WIDE, 1)
    other_stream = lax.ppermute(lax.dynamic_slice_in_dim(residual, SKIP - first, WIDE, 1), "d", OTHER_CORE)
    scale = lax.dynamic_slice_in_dim(layer_scale, first, WIDE, 0).reshape(1, WIDE)
    bias = lax.dynamic_slice_in_dim(out_bias, first, WIDE, 0).reshape(1, WIDE)
    block, own_heads, other_heads, own_stream, other_stream = lax.optimization_barrier(
        (block, own_heads, other_heads, own_stream, other_stream)
    )

    blocks, ranks = [block], [mine]
    for step, step1 in STEPS:
        blocks.append(lax.ppermute(block, "d", moves(step, step1)))
        ranks.append((mine - class_of(*step)) % CLASSES)
    ranks = jnp.stack(ranks).astype(jnp.int32)

    k = ORDER_EARLY
    heads = jnp.concatenate([other_heads, own_heads], axis=1)
    total = early(ranks[:k], heads, blocks[:k])
    other = late(ranks[k:], other_heads, total[:TOK], other_stream, scale, bias, blocks[k:])
    came = lax.ppermute(other, "d", OTHER_CORE)
    own = late(ranks[k:], own_heads, total[TOK:], own_stream, scale, bias, blocks[k:])
    return join(core, own, came)


ORDER_EARLY = 5


def solution(mesh):
    line = Mesh(mesh.devices.reshape(-1), ("d",))
    return jax.shard_map(
        body,
        mesh=line,
        in_specs=(P("d", None), P("d", None), P("d", None), P(), P()),
        out_specs=P("d", None),
        check_vma=False,
    )
```

time: 127 us -> 112 us (0.88)
  matrix products: 14 us -> 2.56 us
  Pallas kernels: 0 us -> 10.9 us
  blocking collectives: 0 us -> 8.71 us
  waiting for transfers between devices: 47.2 us -> 39 us
  starting transfers between devices: 50.4 us -> 44.4 us
  other arithmetic: 5.47 us -> 0.22 us
  local copies, waits for them, and re-layouts: 8.34 us -> 5.41 us
    pallas_call x0 -> x4, Pallas kernels: none -> 10.9 us  [the longest x1 6.04 us: early(): pl.pallas_call(lambda *refs: early_kernel(n, *refs), grid_spec=pltpu.Pref...]
    dot_general x8 -> x0, matrix products: 10.8 us -> none  [body(): jnp.dot(cols.reshape(512, DEPTH), part, preferred_element_type=jnp.float32)]
    all_to_all x1, waiting for transfers between devices: 22.8 us -> 13.8 us  [body(): lax.all_to_all(for_each, 'd', 0, 0, axis_index_groups=GROUPS, tiled=True)]
    all_gather x0 -> x1, blocking collectives: none -> 8.71 us  [body(): lax.all_gather(out_weight, 'd', axis=0, axis_index_groups=CHIP_PAIRS)]
    all_to_all x1, starting transfers between devices: 19.5 us -> 12.1 us  [body(): lax.all_to_all(for_each, 'd', 0, 0, axis_index_groups=GROUPS, tiled=True)]
    another operation x2 -> x1, local copies, waits for them, and re-layouts: 3.57 us -> 0.09 us  [body(): ranks = jnp.stack(ranks).astype(jnp.int32)]
    dynamic_slice x2 -> x4, local copies, waits for them, and re-layouts: 0.16 us -> 2.62 us  [the longest x1 2.44 us: body(): lax.dynamic_slice_in_dim(residual, SKIP - first, WIDE, 1)]
    gather x1 -> x0, local copies, waits for them, and re-layouts: 2.14 us -> none  [body(): for_each = halves[cores]]
  transfers between devices with their start and end apart: 11 -> 11, of which waited for: 5 -> 5; matrix products, arithmetic and copies ran while one was open for 15% -> 6% of each run, Pallas kernels for 0% -> 7%
where the time goes in v2:
time: 112 us
  starting transfers between devices  44.4 us (40%)
  waiting for transfers between devices  39 us (35%)
  Pallas kernels  10.9 us (10%)
  blocking collectives  8.71 us (8%)
  local copies, waits for them, and re-layouts  5.41 us (5%)
  matrix products  2.56 us (2%)
    ppermute x7, starting transfers between devices, body(): blocks.append(lax.ppermute(block, 'd', moves(step, step1)))  23.5 us
    ppermute x7, waiting for transfers between devices, body(): blocks.append(lax.ppermute(block, 'd', moves(step, step1)))  22.8 us
    all_to_all x1, waiting for transfers between devices, body(): lax.all_to_all(for_each, 'd', 0, 0, axis_index_groups=GROUPS, tiled=True)  13.8 us
    all_to_all x1, starting transfers between devices, body(): lax.all_to_all(for_each, 'd', 0, 0, axis_index_groups=GROUPS, tiled=True)  12.1 us
    all_gather x1, blocking collectives, body(): lax.all_gather(out_weight, 'd', axis=0, axis_index_groups=CHIP_PAIRS)  8.71 us
    pallas_call x1, Pallas kernels, early(): pl.pallas_call(lambda *refs: early_kernel(n, *refs), grid_spec=pltpu.Pref...  6.04 us
    ppermute x1, starting transfers between devices, body(): came = lax.ppermute(other, 'd', OTHER_CORE)  4.37 us
    pallas_call x2, Pallas kernels, late(): pl.pallas_call(lambda *refs: late_kernel(n, *refs), grid_spec=pltpu.Prefe...  3.68 us
  transfers between devices with their start and end apart: 11, of which 5 were waited for; matrix products, arithmetic and copies ran while one was open for 6% of the time, Pallas kernels for 7%

profile of v2, /device:TPU:1, one launch (start us, length us, event | category | flops | bytes accessed | tf_op | source)
XLA Modules:
  0.0 111.7 jit_solution(13392664721753109833)
XLA Ops:
  0.0 0.0 copy-start
  0.0 0.0 copy-start.6
  0.0 8.7 %all-gather.1 = bf16[2,4,3200]{2,1,0:T(4,128)(2,1)S(1)} all-gather(bf16[1,4,3200]{2,1,0:T(4,128)(2,1)} %bitcast.20), channel_id=2, replica_groups={{0,64},{1,65},{2,66},{3,67},{4,68},{5,69},{6,70},{7,71},{8,72},{9,73},{..., dimensions={0}, use_global_device_ids=true | all-gather | bytes 76800 | tf_op jit(solution)/shard_map/all_gather | solution.py:185
  8.7 1.0 broadcast_in_dim.8
  9.7 12.1 %all-to-all-start = ((bf16[32,8,1664]{2,1,0:T(8,128)(2,1)}), bf16[32,8,1664]{2,1,0:T(8,128)(2,1)}, u32[]{:S(2)}, u32[]{:S(2)}) async-start(bf16[32,8,1664]{2,1,0:T(8,128)(2,1)} %broadcast_in_dim.8), calls=%async_computation | async-start | bytes 1703936 | tf_op jit(solution)/shard_map/all_to_all | solution.py:188
  21.8 0.0 copy-done
  21.8 0.0 copy-done.6
  21.8 2.6 %fusion.4 = bf16[2048,256]{1,0:T(8,128)(2,1)S(1)} fusion(bf16[256,2048]{1,0:T(8,128)(2,1)S(1)} %copy-done, s32[2048]{0:T(1024)S(1)} %copy-done.6), kind=kOutput, calls=%fused_computation.4 | convolution fusion | flops 2156396544 | bytes 2105344 | tf_op jit(solution)/shard_map/dot_general | solution.py:191
  24.4 0.5 copy.8
  24.9 0.0 copy-start.4
  24.9 0.0 copy-start.5
  24.9 2.5 %collective-permute-start = (bf16[8,256,256]{2,1,0:T(8,128)(2,1)S(1)}, bf16[8,256,256]{2,1,0:T(8,128)(2,1)S(1)}, u32[]{:S(2)}, u32[]{:S(2)}) collective-permute-start(bf16[8,256,256]{2,1,0:T(8,128)(2,1)S(1)} %bitcast.16), channel_id=1, source_target_pairs={{0,64},{1,65},{2,66},{3,67},{4,68},{5,69},{6,70},{7,71},{8,72},{9,... | collective-permute-start | bytes 3145736 | tf_op jit(solution)/shard_map/ppermute | solution.py:193
  27.5 2.4 %constant_dynamic-slice_fusion = (bf16[256,1664]{1,0:T(8,128)(2,1)S(1)}, bf16[256,1664]{1,0:T(8,128)(2,1)}) fusion(bf16[256,3200]{1,0:T(8,128)(2,1)} %param.6, s32[]{:T(128)S(6)} %select_n.86, s32[]{:T(128)S(6)} %select_n.85), kind=kLoop, calls=%fused_computation.6 | loop fusion | bytes 3407880 | tf_op jit(solution)/shard_map/dynamic_slice | solution.py:195
  29.9 1.9 %collective-permute-start.1 = (bf16[256,1664]{1,0:T(8,128)(2,1)S(1)}, bf16[256,1664]{1,0:T(8,128)(2,1)S(1)}, u32[]{:S(2)}, u32[]{:S(2)}) collective-permute-start(bf16[256,1664]{1,0:T(8,128)(2,1)S(1)} %get-tuple-element.17), channel_id=1, source_target_pairs={{0,64},{1,65},{2,66},{3,67},{4,68},{5,69},{6,70},{7,71},{8,72},{9,... | collective-permute-start | bytes 2555912 | tf_op jit(solution)/shard_map/ppermute | solution.py:195
  31.9 2.3 %collective-permute-done.1.refs_3_ = bf16[256,1664]{1,0:T(8,128)(2,1)S(1)} collective-permute-done((bf16[256,1664]{1,0:T(8,128)(2,1)S(1)}, bf16[256,1664]{1,0:T(8,128)(2,1)S(1)}, u32[]{:S(2)}, u32[]{:S(2)}) %collective-permute-start.1) | collective-permute-done | bytes 852000 | tf_op jit(solution)/shard_map/ppermute | solution.py:195
  34.2 0.0 copy-start.2
  34.2 0.9 copy-done.2
  35.1 0.0 collective-permute-done.refs_1_
  35.1 13.8 %all-to-all-done = bf16[32,8,1664]{2,1,0:T(8,128)(2,1)} async-done(((bf16[32,8,1664]{2,1,0:T(8,128)(2,1)}), bf16[32,8,1664]{2,1,0:T(8,128)(2,1)}, u32[]{:S(2)}, u32[]{:S(2)}) %all-to-all-start) | async-done | bytes 852000 | tf_op jit(solution)/shard_map/all_to_all | solution.py:188
  48.9 2.7 %collective-permute-start.2 = (bf16[256,1664]{1,0:T(8,128)(2,1)}, bf16[256,1664]{1,0:T(8,128)(2,1)}, u32[]{:S(2)}, u32[]{:S(2)}) collective-permute-start(bf16[256,1664]{1,0:T(8,128)(2,1)} %bitcast.5.refs_2_), channel_id=1, source_target_pairs={{0,8},{1,9},{2,10},{3,11},{4,12},{5,13},{6,14},{7,15},{8,16},{9,17... | collective-permute-start | bytes 2555912 | tf_op jit(solution)/shard_map/ppermute | solution.py:204
  51.6 3.8 %collective-permute-start.3 = (bf16[256,1664]{1,0:T(8,128)(2,1)}, bf16[256,1664]{1,0:T(8,128)(2,1)}, u32[]{:S(2)}, u32[]{:S(2)}) collective-permute-start(bf16[256,1664]{1,0:T(8,128)(2,1)} %bitcast.5.refs_2_), channel_id=1, source_target_pairs={{0,24},{1,25},{2,26},{3,27},{4,28},{5,29},{6,30},{7,31},{8,0},{9,1... | collective-permute-start | bytes 2555912 | tf_op jit(solution)/shard_map/ppermute | solution.py:204
  55.4 2.8 %collective-permute-start.4 = (bf16[256,1664]{1,0:T(8,128)(2,1)}, bf16[256,1664]{1,0:T(8,128)(2,1)}, u32[]{:S(2)}, u32[]{:S(2)}) collective-permute-start(bf16[256,1664]{1,0:T(8,128)(2,1)} %bitcast.5.refs_2_), channel_id=1, source_target_pairs={{0,32},{1,33},{2,34},{3,35},{4,36},{5,37},{6,38},{7,39},{8,40},{9,... | collective-permute-start | bytes 2555912 | tf_op jit(solution)/shard_map/ppermute | solution.py:204
  58.2 3.7 %collective-permute-start.5 = (bf16[256,1664]{1,0:T(8,128)(2,1)}, bf16[256,1664]{1,0:T(8,128)(2,1)}, u32[]{:S(2)}, u32[]{:S(2)}) collective-permute-start(bf16[256,1664]{1,0:T(8,128)(2,1)} %bitcast.5.refs_2_), channel_id=1, source_target_pairs={{0,416},{1,417},{2,418},{3,419},{4,420},{5,421},{6,422},{7,423},{8... | collective-permute-start | bytes 2555912 | tf_op jit(solution)/shard_map/ppermute | solution.py:204
  62.1 0.0 copy-done.4
  62.1 0.1 dynamic_slice.18
  62.2 0.0 copy-done.5
  62.2 0.1 dynamic_slice.19
  62.3 0.1 stack.38.refs_0_
  62.4 0.1 pad_add_fusion.refs_0_
  62.5 3.6 %collective-permute-start.6 = (bf16[256,1664]{1,0:T(8,128)(2,1)}, bf16[256,1664]{1,0:T(8,128)(2,1)S(1)}, u32[]{:S(2)}, u32[]{:S(2)}) collective-permute-start(bf16[256,1664]{1,0:T(8,128)(2,1)} %bitcast.5.refs_2_), channel_id=1, source_target_pairs={{0,1},{1,2},{2,3},{3,4},{4,5},{5,6},{6,7},{7,0},{8,9},{9,10},{10,1... | collective-permute-start | bytes 2555912 | tf_op jit(solution)/shard_map/ppermute | solution.py:204
  66.1 4.3 %collective-permute-done.2.refs_3_ = bf16[256,1664]{1,0:T(8,128)(2,1)} collective-permute-done((bf16[256,1664]{1,0:T(8,128)(2,1)}, bf16[256,1664]{1,0:T(8,128)(2,1)}, u32[]{:S(2)}, u32[]{:S(2)}) %collective-permute-start.2) | collective-permute-done | bytes 852000 | tf_op jit(solution)/shard_map/ppermute | solution.py:204
  70.4 5.0 %collective-permute-start.7 = (bf16[256,1664]{1,0:T(8,128)(2,1)}, bf16[256,1664]{1,0:T(8,128)(2,1)S(1)}, u32[]{:S(2)}, u32[]{:S(2)}) collective-permute-start(bf16[256,1664]{1,0:T(8,128)(2,1)} %bitcast.5.refs_2_), channel_id=1, source_target_pairs={{0,7},{1,0},{2,1},{3,2},{4,3},{5,4},{6,5},{7,6},{8,15},{9,8},{10,9... | collective-permute-start | bytes 2555912 | tf_op jit(solution)/shard_map/ppermute | solution.py:204
  75.4 0.0 collective-permute-done.3.refs_4_
  75.4 2.0 %collective-permute-start.8 = (bf16[256,1664]{1,0:T(8,128)(2,1)}, bf16[256,1664]{1,0:T(8,128)(2,1)S(1)}, u32[]{:S(2)}, u32[]{:S(2)}) collective-permute-start(bf16[256,1664]{1,0:T(8,128)(2,1)} %bitcast.5.refs_2_), channel_id=1, source_target_pairs={{0,33},{1,34},{2,35},{3,36},{4,37},{5,38},{6,39},{7,32},{8,41},{9,... | collective-permute-start | bytes 2555912 | tf_op jit(solution)/shard_map/ppermute | solution.py:204
  77.3 0.1 pad_maximum_fusion.refs_1_
  77.5 0.0 collective-permute-done.4.refs_5_
  77.5 0.0 collective-permute-done.5.refs_6_
  77.5 6.0 %shard_map.64 = f32[512,1664]{1,0:T(8,128)S(1)} custom-call(s32[5]{0:T(128)S(1)} %stack.38.refs_0_, bf16[8,512,256]{2,1,0:T(8,128)(2,1)S(1)} %pad_maximum_fusion.refs_1_, bf16[256,1664]{1,0:T(8,128)(2,1)} %bitcast.5.refs_2_, bf16[256,1664]{1,0:T(8,128)(2,1)} %collective-permute-done.2.refs_3_, bf16[256,1664]{1,0:T(8,128)(2,1)} %collective-permute-done.3.refs_4_, ...), custom_call_target="tpu_custom_call" | custom-call | flops 2181038080 | bytes 8388608 | tf_op jit(solution)/shard_map/pallas_call | solution.py:122
  83.6 0.0 copy-start.3
  83.6 0.2 fusion.7
  83.8 0.0 collective-permute-done.6.refs_6_
  83.8 18.5 %collective-permute-done.7.refs_7_ = bf16[256,1664]{1,0:T(8,128)(2,1)S(1)} collective-permute-done((bf16[256,1664]{1,0:T(8,128)(2,1)}, bf16[256,1664]{1,0:T(8,128)(2,1)S(1)}, u32[]{:S(2)}, u32[]{:S(2)}) %collective-permute-start.7) | collective-permute-done | bytes 852000 | tf_op jit(solution)/shard_map/ppermute | solution.py:204
  102.3 0.0 collective-permute-done.8.refs_8_
  102.3 0.0 copy-done.3
  102.3 0.0 copy-start.1
  102.3 1.8 %shard_map.66 = bf16[256,1664]{1,0:T(8,128)(2,1)S(1)} custom-call(s32[3]{0:T(128)S(1)} %pad_add_fusion.refs_0_, bf16[8,256,256]{2,1,0:T(8,128)(2,1)S(1)} %collective-permute-done.refs_1_, f32[256,1664]{1,0:T(8,128)S(1)} %get-tuple-element.15.refs_2_, bf16[256,1664]{1,0:T(8,128)(2,1)S(1)} %copy-done.3, f32[1,1664]{1,0:T(1,128)S(1)} %reshape.20.refs_4_, ...), custom_call_target="tpu_custom_call" | custom-call | flops 654311424 | bytes 4194304 | tf_op jit(solution)/shard_map/pallas_call | solution.py:140
  104.1 4.4 %collective-permute-start.9 = (bf16[256,1664]{1,0:T(8,128)(2,1)S(1)}, bf16[256,1664]{1,0:T(8,128)(2,1)S(1)}, u32[]{:S(2)}, u32[]{:S(2)}) collective-permute-start(bf16[256,1664]{1,0:T(8,128)(2,1)S(1)} %shard_map.66), channel_id=1, source_target_pairs={{0,64},{1,65},{2,66},{3,67},{4,68},{5,69},{6,70},{7,71},{8,72},{9,... | collective-permute-start | bytes 2555912 | tf_op jit(solution)/shard_map/ppermute | solution.py:212
  108.5 0.0 copy-done.1
  108.5 1.8 %shard_map.65.own_ref = bf16[256,1664]{1,0:T(8,128)(2,1)S(1)} custom-call(s32[3]{0:T(128)S(1)} %pad_add_fusion.refs_0_, bf16[8,256,256]{2,1,0:T(8,128)(2,1)S(1)} %bitcast.18, f32[256,1664]{1,0:T(8,128)S(1)} %get-tuple-element.16.refs_2_, bf16[256,1664]{1,0:T(8,128)(2,1)S(1)} %copy-done.1, f32[1,1664]{1,0:T(1,128)S(1)} %reshape.20.refs_4_, ...), custom_call_target="tpu_custom_call" | custom-call | flops 654311424 | bytes 4194304 | tf_op jit(solution)/shard_map/pallas_call | solution.py:140
  110.4 0.1 collective-permute-done.9.other_ref
  110.5 1.2 %shard_map.67 = bf16[256,3200]{1,0:T(8,128)(2,1)} custom-call(s32[1]{0:T(128)} %bitcast.core_ref, bf16[256,1664]{1,0:T(8,128)(2,1)S(1)} %shard_map.65.own_ref, bf16[256,1664]{1,0:T(8,128)(2,1)S(1)} %collective-permute-done.9.other_ref), custom_call_target="tpu_custom_call" | custom-call | tf_op jit(solution)/shard_map/pallas_call | solution.py:163
  (4 shorter events, 0.0 us)
Async XLA Ops:
  0.0 21.8 %copy-start = (bf16[256,2048]{1,0:T(8,128)(2,1)S(1)}, bf16[256,2048]{1,0:T(8,128)(2,1)}, u32[]{:S(2)}) copy-start(bf16[256,2048]{1,0:T(8,128)(2,1)} %param.7) | copy-start | bytes 3145732
  0.0 21.8 %copy-start.6 = (s32[2048]{0:T(1024)S(1)}, s32[2048]{0:T(1024)}, u32[]{:S(2)}) copy-start(s32[2048]{0:T(1024)} %constant.147) | copy-start | bytes 24580
  9.7 39.2 %all-to-all-start = ((bf16[32,8,1664]{2,1,0:T(8,128)(2,1)}), bf16[32,8,1664]{2,1,0:T(8,128)(2,1)}, u32[]{:S(2)}, u32[]{:S(2)}) async-start(bf16[32,8,1664]{2,1,0:T(8,128)(2,1)} %broadcast_in_dim.8), calls=%async_computation | async-start | bytes 1703936 | tf_op jit(solution)/shard_map/all_to_all | solution.py:188
  24.9 37.2 %copy-start.4 = (f32[3200]{0:T(1024)S(1)}, f32[3200]{0:T(1024)}, u32[]{:S(2)}) copy-start(f32[3200]{0:T(1024)} %param.10) | copy-start | bytes 38404
  24.9 37.3 %copy-start.5 = (f32[3200]{0:T(1024)S(1)}, f32[3200]{0:T(1024)}, u32[]{:S(2)}) copy-start(f32[3200]{0:T(1024)} %param.9) | copy-start | bytes 38404
  24.9 10.2 %collective-permute-start = (bf16[8,256,256]{2,1,0:T(8,128)(2,1)S(1)}, bf16[8,256,256]{2,1,0:T(8,128)(2,1)S(1)}, u32[]{:S(2)}, u32[]{:S(2)}) collective-permute-start(bf16[8,256,256]{2,1,0:T(8,128)(2,1)S(1)} %bitcast.16), channel_id=1, source_target_pairs={{0,64},{1,65},{2,66},{3,67},{4,68},{5,69},{6,70},{7,71},{8,72},{9,... | collective-permute-start | bytes 3145736 | tf_op jit(solution)/shard_map/ppermute | solution.py:193
  29.9 4.3 %collective-permute-start.1 = (bf16[256,1664]{1,0:T(8,128)(2,1)S(1)}, bf16[256,1664]{1,0:T(8,128)(2,1)S(1)}, u32[]{:S(2)}, u32[]{:S(2)}) collective-permute-start(bf16[256,1664]{1,0:T(8,128)(2,1)S(1)} %get-tuple-element.17), channel_id=1, source_target_pairs={{0,64},{1,65},{2,66},{3,67},{4,68},{5,69},{6,70},{7,71},{8,72},{9,... | collective-permute-start | bytes 2555912 | tf_op jit(solution)/shard_map/ppermute | solution.py:195
  34.2 0.9 copy-start.2
  48.9 21.4 %collective-permute-start.2 = (bf16[256,1664]{1,0:T(8,128)(2,1)}, bf16[256,1664]{1,0:T(8,128)(2,1)}, u32[]{:S(2)}, u32[]{:S(2)}) collective-permute-start(bf16[256,1664]{1,0:T(8,128)(2,1)} %bitcast.5.refs_2_), channel_id=1, source_target_pairs={{0,8},{1,9},{2,10},{3,11},{4,12},{5,13},{6,14},{7,15},{8,16},{9,17... | collective-permute-start | bytes 2555912 | tf_op jit(solution)/shard_map/ppermute | solution.py:204
  51.6 23.7 %collective-permute-start.3 = (bf16[256,1664]{1,0:T(8,128)(2,1)}, bf16[256,1664]{1,0:T(8,128)(2,1)}, u32[]{:S(2)}, u32[]{:S(2)}) collective-permute-start(bf16[256,1664]{1,0:T(8,128)(2,1)} %bitcast.5.refs_2_), channel_id=1, source_target_pairs={{0,24},{1,25},{2,26},{3,27},{4,28},{5,29},{6,30},{7,31},{8,0},{9,1... | collective-permute-start | bytes 2555912 | tf_op jit(solution)/shard_map/ppermute | solution.py:204
  55.4 22.1 %collective-permute-start.4 = (bf16[256,1664]{1,0:T(8,128)(2,1)}, bf16[256,1664]{1,0:T(8,128)(2,1)}, u32[]{:S(2)}, u32[]{:S(2)}) collective-permute-start(bf16[256,1664]{1,0:T(8,128)(2,1)} %bitcast.5.refs_2_), channel_id=1, source_target_pairs={{0,32},{1,33},{2,34},{3,35},{4,36},{5,37},{6,38},{7,39},{8,40},{9,... | collective-permute-start | bytes 2555912 | tf_op jit(solution)/shard_map/ppermute | solution.py:204
  58.2 19.3 %collective-permute-start.5 = (bf16[256,1664]{1,0:T(8,128)(2,1)}, bf16[256,1664]{1,0:T(8,128)(2,1)}, u32[]{:S(2)}, u32[]{:S(2)}) collective-permute-start(bf16[256,1664]{1,0:T(8,128)(2,1)} %bitcast.5.refs_2_), channel_id=1, source_target_pairs={{0,416},{1,417},{2,418},{3,419},{4,420},{5,421},{6,422},{7,423},{8... | collective-permute-start | bytes 2555912 | tf_op jit(solution)/shard_map/ppermute | solution.py:204
  62.5 21.3 %collective-permute-start.6 = (bf16[256,1664]{1,0:T(8,128)(2,1)}, bf16[256,1664]{1,0:T(8,128)(2,1)S(1)}, u32[]{:S(2)}, u32[]{:S(2)}) collective-permute-start(bf16[256,1664]{1,0:T(8,128)(2,1)} %bitcast.5.refs_2_), channel_id=1, source_target_pairs={{0,1},{1,2},{2,3},{3,4},{4,5},{5,6},{6,7},{7,0},{8,9},{9,10},{10,1... | collective-permute-start | bytes 2555912 | tf_op jit(solution)/shard_map/ppermute | solution.py:204
  70.4 31.9 %collective-permute-start.7 = (bf16[256,1664]{1,0:T(8,128)(2,1)}, bf16[256,1664]{1,0:T(8,128)(2,1)S(1)}, u32[]{:S(2)}, u32[]{:S(2)}) collective-permute-start(bf16[256,1664]{1,0:T(8,128)(2,1)} %bitcast.5.refs_2_), channel_id=1, source_target_pairs={{0,7},{1,0},{2,1},{3,2},{4,3},{5,4},{6,5},{7,6},{8,15},{9,8},{10,9... | collective-permute-start | bytes 2555912 | tf_op jit(solution)/shard_map/ppermute | solution.py:204
  75.4 26.9 %collective-permute-start.8 = (bf16[256,1664]{1,0:T(8,128)(2,1)}, bf16[256,1664]{1,0:T(8,128)(2,1)S(1)}, u32[]{:S(2)}, u32[]{:S(2)}) collective-permute-start(bf16[256,1664]{1,0:T(8,128)(2,1)} %bitcast.5.refs_2_), channel_id=1, source_target_pairs={{0,33},{1,34},{2,35},{3,36},{4,37},{5,38},{6,39},{7,32},{8,41},{9,... | collective-permute-start | bytes 2555912 | tf_op jit(solution)/shard_map/ppermute | solution.py:204
  83.6 18.7 %copy-start.3 = (bf16[256,1664]{1,0:T(8,128)(2,1)S(1)}, bf16[256,1664]{1,0:T(8,128)(2,1)}, u32[]{:S(2)}) copy-start(bf16[256,1664]{1,0:T(8,128)(2,1)} %copy-done.2) | copy-start | bytes 2555908
  102.3 6.2 %copy-start.1 = (bf16[256,1664]{1,0:T(8,128)(2,1)S(1)}, bf16[256,1664]{1,0:T(8,128)(2,1)}, u32[]{:S(2)}) copy-start(bf16[256,1664]{1,0:T(8,128)(2,1)} %get-tuple-element.13.refs_3_) | copy-start | bytes 2555908
  104.1 6.4 %collective-permute-start.9 = (bf16[256,1664]{1,0:T(8,128)(2,1)S(1)}, bf16[256,1664]{1,0:T(8,128)(2,1)S(1)}, u32[]{:S(2)}, u32[]{:S(2)}) collective-permute-start(bf16[256,1664]{1,0:T(8,128)(2,1)S(1)} %shard_map.66), channel_id=1, source_target_pairs={{0,64},{1,65},{2,66},{3,67},{4,68},{5,69},{6,70},{7,71},{8,72},{9,... | collective-permute-start | bytes 2555912 | tf_op jit(solution)/shard_map/ppermute | solution.py:212

commit v3 on v2

v3 whole, which is shorter than its diff:
```python
import functools

import jax
import jax.numpy as jnp
import numpy as np
from jax import lax
from jax.experimental import pallas as pl
from jax.experimental.pallas import tpu as pltpu
from jax.sharding import Mesh, PartitionSpec as P

D = 3200
INNER = 2048
TOK = 256
WIDE = 1664
SKIP = D - WIDE
Y, CORES, X, Z = 8, 2, 4, 8
CLASSES = 8
ROWS = 4
DEPTH = INNER // CLASSES
MIB = 1 << 20


def index_of(core, x, y, z):
    y, x, z = y % Y, x % X, z % Z
    return (((y // 2 * CORES + core) * 2 + y % 2) * X + x) * Z + z


def places():
    for core in range(CORES):
        for y in range(Y):
            for x in range(X):
                for z in range(Z):
                    yield core, x, y, z


def class_of(x, y, z):
    return (2 * x + y + 3 * z) % CLASSES


def class_chips():
    chips = [[] for _ in range(CLASSES)]
    for core, x, y, z in places():
        if core == 0:
            chips[class_of(x, y, z)].append((x, y, z))
    return chips


def moves(step, step1=None):
    pairs = []
    for core, x, y, z in places():
        ex, ey, ez = step1 if core and step1 else step
        pairs.append((index_of(core, x, y, z), index_of(core, x + ex, y + ey, z + ez)))
    return pairs


CHIPS = class_chips()
GROUPS = [[index_of(core, *chip) for chip in chips] for core in range(CORES) for chips in CHIPS]
CHIP_PAIRS = [[index_of(0, x, y, z), index_of(1, x, y, z)] for core, x, y, z in places() if core == 0]
OTHER_CORE = [(index_of(c, x, y, z), index_of(1 - c, x, y, z)) for c, x, y, z in places()]
ORDER = np.array(
    [
        index_of(core, *chip) * ROWS + i
        for chips in CHIPS
        for chip in chips
        for core in range(CORES)
        for i in range(ROWS)
    ],
    np.int32,
)
STEPS = [
    ((1, 0, 0), (-1, 0, 0)),
    ((0, 1, 1), (0, -1, -1)),
    ((0, 1, 0), (0, -1, 0)),
    ((0, 0, 1), (0, 0, -1)),
    ((-1, 0, 0), (1, 0, 0)),
    ((0, -1, 0), (0, 1, 0)),
    ((0, 0, -1), (0, 0, 1)),
]

def fetch(block_refs, slots, sems):
    copies = [pltpu.make_async_copy(ref, slots.at[k], sems.at[k]) for k, ref in enumerate(block_refs)]
    for copy in copies:
        copy.start()
    return copies


def early_kernel(n, rank_ref, heads_ref, *refs):
    block_refs, so_far_ref, (total_ref, slots, sems) = refs[:n], refs[n:-3], refs[-3:]
    copies = fetch(block_refs, slots, sems)
    for copy in copies:
        copy.wait()
    for columns in TILES:
        total = so_far_ref[0][:, columns] if so_far_ref else 0.0
        for k in range(n):
            part = slots[k, :, columns]
            total = total + jnp.dot(heads_ref[rank_ref[k]], part, preferred_element_type=jnp.float32)
        total_ref[:, columns] = total


def late_kernel(rows, rank_ref, heads_ref, so_far_ref, stream_ref, scale_ref, bias_ref, *refs):
    *block_refs, out_ref, slots, sems = refs
    copies = fetch(block_refs, slots, sems)
    for copy in copies:
        copy.wait()
    for columns in TILES:
        total = so_far_ref[rows, columns]
        for k in range(len(copies)):
            part = slots[k, :, columns]
            total = total + jnp.dot(heads_ref[rank_ref[k], rows], part, preferred_element_type=jnp.float32)
        branch = scale_ref[:, columns] * (total + bias_ref[:, columns])
        out_ref[:, columns] = (stream_ref[:, columns].astype(jnp.float32) + branch).astype(jnp.bfloat16)


TILES = [slice(c, min(c + 512, WIDE)) for c in range(0, WIDE, 512)]
VMEM_SPEC = pl.BlockSpec(memory_space=pltpu.VMEM)
SMEM_SPEC = pl.BlockSpec(memory_space=pltpu.SMEM)
ANY_SPEC = pl.BlockSpec(memory_space=pl.ANY)


def slots_for(n):
    return [pltpu.VMEM((n, DEPTH, WIDE), jnp.bfloat16), pltpu.SemaphoreType.DMA((n,))]


def cost(n, rows):
    return pl.CostEstimate(flops=2 * rows * n * DEPTH * WIDE, bytes_accessed=n * DEPTH * WIDE * 2, transcendentals=0)


def early(ranks, heads, blocks, *so_far):
    n = len(blocks)
    return pl.pallas_call(
        functools.partial(early_kernel, n),
        in_specs=[SMEM_SPEC, VMEM_SPEC] + [ANY_SPEC] * n + [VMEM_SPEC] * len(so_far),
        out_specs=VMEM_SPEC,
        out_shape=jax.ShapeDtypeStruct((2 * TOK, WIDE), jnp.float32),
        scratch_shapes=slots_for(n),
        compiler_params=pltpu.CompilerParams(vmem_limit_bytes=24 * MIB),
        cost_estimate=cost(n, 2 * TOK),
    )(ranks, heads, *blocks, *so_far)


def late(half, ranks, heads, so_far, stream, scale, bias, blocks):
    n = len(blocks)
    return pl.pallas_call(
        functools.partial(late_kernel, slice(half * TOK, (half + 1) * TOK)),
        in_specs=[SMEM_SPEC] + [VMEM_SPEC] * 5 + [ANY_SPEC] * n,
        out_specs=VMEM_SPEC,
        out_shape=jax.ShapeDtypeStruct((TOK, WIDE), jnp.bfloat16),
        scratch_shapes=slots_for(n),
        compiler_params=pltpu.CompilerParams(vmem_limit_bytes=24 * MIB),
        cost_estimate=cost(n, TOK),
    )(ranks, heads, so_far, stream, scale, bias, *blocks)


def join_kernel(core_ref, own_ref, other_ref, out_ref):
    @pl.when(core_ref[0] == 0)
    def _():
        out_ref[:, :WIDE] = own_ref[...]
        out_ref[:, WIDE:] = other_ref[:, WIDE - SKIP :]

    @pl.when(core_ref[0] == 1)
    def _():
        out_ref[:, :SKIP] = other_ref[:, :SKIP]
        out_ref[:, SKIP:] = own_ref[...]


def join(core, own, other):
    tile = TOK // 2
    return pl.pallas_call(
        join_kernel,
        grid_spec=pltpu.PrefetchScalarGridSpec(
            num_scalar_prefetch=1,
            grid=(2,),
            in_specs=[pl.BlockSpec((tile, WIDE), lambda i, *_: (i, 0))] * 2,
            out_specs=pl.BlockSpec((tile, D), lambda i, *_: (i, 0)),
        ),
        out_shape=jax.ShapeDtypeStruct((TOK, D), jnp.bfloat16),
        compiler_params=pltpu.CompilerParams(vmem_limit_bytes=16 * MIB),
    )(core.reshape(1), own, other)


def rise(core, step, step1):
    return class_of(*step) + core * (class_of(*step1) - class_of(*step))


def body(residual, heads_out, out_weight, out_bias, layer_scale):
    me = lax.axis_index("d")
    core = me // (2 * X * Z) % CORES
    z = me % Z
    x = me // Z % X
    y = me // (CORES * 2 * X * Z) * 2 + me // (X * Z) % 2
    mine = class_of(x, y, z)
    first = core * SKIP

    chip_rows = lax.all_gather(out_weight, "d", axis=0, axis_index_groups=CHIP_PAIRS)
    chip_rows = lax.dynamic_slice_in_dim(chip_rows, first, WIDE, 2).reshape(1, CORES * ROWS, WIDE)
    for_each = jnp.broadcast_to(chip_rows, (len(CHIPS[0]), CORES * ROWS, WIDE))
    block = lax.all_to_all(for_each, "d", 0, 0, axis_index_groups=GROUPS, tiled=True).reshape(DEPTH, WIDE)

    pick = (lax.broadcasted_iota(jnp.int32, (INNER, INNER), 0) == ORDER[None, :]).astype(jnp.bfloat16)
    own_heads = jnp.dot(heads_out, pick, preferred_element_type=jnp.float32).astype(jnp.bfloat16)
    own_heads = own_heads.reshape(TOK, CLASSES, DEPTH).transpose(1, 0, 2)
    other_heads = lax.ppermute(own_heads, "d", OTHER_CORE)
    own_stream = lax.dynamic_slice_in_dim(residual, first, WIDE, 1)
    other_stream = lax.ppermute(lax.dynamic_slice_in_dim(residual, SKIP - first, WIDE, 1), "d", OTHER_CORE)
    scale = lax.dynamic_slice_in_dim(layer_scale, first, WIDE, 0).reshape(1, WIDE)
    bias = lax.dynamic_slice_in_dim(out_bias, first, WIDE, 0).reshape(1, WIDE)
    heads = jnp.concatenate([other_heads, own_heads], axis=1)
    block, heads, own_stream, other_stream = lax.optimization_barrier((block, heads, own_stream, other_stream))

    ranks = jnp.stack([mine] + [(mine - rise(core, *step)) % CLASSES for step in STEPS]).astype(jnp.int32)
    blocks = [block] + [lax.ppermute(block, "d", moves(*step)) for step in STEPS[:AHEAD]]
    total = early(ranks[:FIRST], heads, blocks[:FIRST])
    block, total = lax.optimization_barrier((block, total))
    blocks += [lax.ppermute(block, "d", moves(*step)) for step in STEPS[AHEAD:]]
    total = early(ranks[FIRST:SOON], heads, blocks[FIRST:SOON], total)
    last = (ranks[SOON:], heads, total)
    other = late(0, *last, other_stream, scale, bias, blocks[SOON:])
    came = lax.ppermute(other, "d", OTHER_CORE)
    own = late(1, *last, own_stream, scale, bias, blocks[SOON:])
    return join(core, own, came)


FIRST = 1
AHEAD = 5
SOON = 6


def solution(mesh):
    line = Mesh(mesh.devices.reshape(-1), ("d",))
    return jax.shard_map(
        body,
        mesh=line,
        in_specs=(P("d", None), P("d", None), P("d", None), P(), P()),
        out_specs=P("d", None),
        check_vma=False,
    )
```

time: 112 us -> 102 us (0.911)
  waiting for transfers between devices: 39 us -> 19.4 us
  local copies, waits for them, and re-layouts: 5.41 us -> 8.85 us
  Pallas kernels: 10.9 us -> 13.8 us
  other arithmetic: 0.22 us -> 1.76 us
    ppermute x7, waiting for transfers between devices: 22.8 us -> 5.6 us  [the longest x2 3.1 us: body(): blocks += [lax.ppermute(block, 'd', moves(*step)) for step in STEPS[AHEAD:]]]
    unnamed x14 -> x18, local copies, waits for them, and re-layouts: 0.97 us -> 4.6 us
    pallas_call x3 -> x4, Pallas kernels: 9.72 us -> 12.5 us  [the longest x2 7.16 us: early(): pl.pallas_call(functools.partial(early_kernel, n), in_specs=[SMEM_SPEC, V...]
    ppermute x1, waiting for transfers between devices: 2.34 us -> 0.61 us  [body(): lax.ppermute(lax.dynamic_slice_in_dim(residual, SKIP - first, WIDE, 1), '...]
    concatenate x1, other arithmetic: 0.15 us -> 1.68 us  [body(): heads = jnp.concatenate([other_heads, own_heads], axis=1)]
  transfers between devices with their start and end apart: 11 -> 11, of which waited for: 5 -> 6; matrix products, arithmetic and copies ran while one was open for 6% -> 8% of each run, Pallas kernels for 7% -> 10%
where the time goes in v3:
time: 102 us; the launch traced here: 101 us
  starting transfers between devices  45.1 us (44%)
  waiting for transfers between devices  19.4 us (19%)
  Pallas kernels  13.8 us (14%)
  local copies, waits for them, and re-layouts  8.85 us (9%)
  blocking collectives  8.71 us (9%)
  matrix products  3.25 us (3%)
  other arithmetic  1.76 us (2%)
    ppermute x5, starting transfers between devices, body(): lax.ppermute(block, 'd', moves(*step))  18.6 us
    all_to_all x1, waiting for transfers between devices, body(): lax.all_to_all(for_each, 'd', 0, 0, axis_index_groups=GROUPS, tiled=True)  13.2 us
    all_to_all x1, starting transfers between devices, body(): lax.all_to_all(for_each, 'd', 0, 0, axis_index_groups=GROUPS, tiled=True)  12.1 us
    all_gather x1, blocking collectives, body(): lax.all_gather(out_weight, 'd', axis=0, axis_index_groups=CHIP_PAIRS)  8.71 us
    pallas_call x2, Pallas kernels, early(): pl.pallas_call(functools.partial(early_kernel, n), in_specs=[SMEM_SPEC, V...  7.16 us
    pallas_call x2, Pallas kernels, late(): pl.pallas_call(functools.partial(late_kernel, slice(half * TOK, (half + 1...  5.37 us
    ppermute x2, starting transfers between devices, body(): blocks += [lax.ppermute(block, 'd', moves(*step)) for step in STEPS[AHEAD:]]  5.27 us
    ppermute x1, starting transfers between devices, body(): came = lax.ppermute(other, 'd', OTHER_CORE)  4.75 us
  transfers between devices with their start and end apart: 11, of which 6 were waited for; matrix products, arithmetic and copies ran while one was open for 8% of the time, Pallas kernels for 10%

profile of v3, /device:TPU:1, one launch (start us, length us, event | category | flops | bytes accessed | tf_op | source)
XLA Modules:
  0.0 101.3 jit_solution(4989682721033197508)
XLA Ops:
  0.0 0.0 copy-start
  0.0 8.7 %all-gather.1 = bf16[2,4,3200]{2,1,0:T(4,128)(2,1)S(1)} all-gather(bf16[1,4,3200]{2,1,0:T(4,128)(2,1)} %bitcast.19), channel_id=2, replica_groups={{0,64},{1,65},{2,66},{3,67},{4,68},{5,69},{6,70},{7,71},{8,72},{9,73},{..., dimensions={0}, use_global_device_ids=true | all-gather | bytes 76800 | tf_op jit(solution)/shard_map/all_gather | solution.py:194
  8.7 1.0 broadcast_in_dim.8
  9.7 12.1 %all-to-all-start = ((bf16[32,8,1664]{2,1,0:T(8,128)(2,1)}), bf16[32,8,1664]{2,1,0:T(8,128)(2,1)}, u32[]{:S(2)}, u32[]{:S(2)}) async-start(bf16[32,8,1664]{2,1,0:T(8,128)(2,1)} %broadcast_in_dim.8), calls=%async_computation | async-start | bytes 1703936 | tf_op jit(solution)/shard_map/all_to_all | solution.py:197
  21.8 0.0 copy-done
  21.8 3.3 %fusion.4 = bf16[2048,256]{1,0:T(8,128)(2,1)S(1)} fusion(bf16[256,2048]{1,0:T(8,128)(2,1)S(1)} %copy-done, s32[2048]{0:T(1024)} %constant.141), kind=kOutput, calls=%fused_computation.4 | convolution fusion | flops 2156396544 | bytes 2105344 | tf_op jit(solution)/shard_map/dot_general | solution.py:200
  25.1 0.5 copy.8
  25.6 0.0 copy-start.6
  25.6 2.5 %collective-permute-start = (bf16[8,256,256]{2,1,0:T(8,128)(2,1)S(1)}, bf16[8,256,256]{2,1,0:T(8,128)(2,1)}, u32[]{:S(2)}, u32[]{:S(2)}) collective-permute-start(bf16[8,256,256]{2,1,0:T(8,128)(2,1)S(1)} %bitcast.16), channel_id=1, source_target_pairs={{0,64},{1,65},{2,66},{3,67},{4,68},{5,69},{6,70},{7,71},{8,72},{9,... | collective-permute-start | bytes 3145736 | tf_op jit(solution)/shard_map/ppermute | solution.py:202
  28.2 2.4 %constant_dynamic-slice_fusion = (bf16[256,1664]{1,0:T(8,128)(2,1)S(1)}, bf16[256,1664]{1,0:T(8,128)(2,1)}) fusion(bf16[256,3200]{1,0:T(8,128)(2,1)} %param.6, s32[]{:T(128)S(6)} %select_n.85, s32[]{:T(128)S(6)} %select_n.84), kind=kLoop, calls=%fused_computation.6 | loop fusion | bytes 3407880 | tf_op jit(solution)/shard_map/dynamic_slice | solution.py:204
  30.6 1.9 %collective-permute-start.1 = (bf16[256,1664]{1,0:T(8,128)(2,1)S(1)}, bf16[256,1664]{1,0:T(8,128)(2,1)S(1)}, u32[]{:S(2)}, u32[]{:S(2)}) collective-permute-start(bf16[256,1664]{1,0:T(8,128)(2,1)S(1)} %get-tuple-element.17), channel_id=1, source_target_pairs={{0,64},{1,65},{2,66},{3,67},{4,68},{5,69},{6,70},{7,71},{8,72},{9,... | collective-permute-start | bytes 2555912 | tf_op jit(solution)/shard_map/ppermute | solution.py:204
  32.5 0.0 copy-done.6
  32.6 0.0 collective-permute-done
  32.6 1.7 %pad_maximum_fusion.heads_ref = bf16[8,512,256]{2,1,0:T(8,128)(2,1)S(1)} fusion(bf16[8,256,256]{2,1,0:T(8,128)(2,1)} %bitcast.17, bf16[8,256,256]{2,1,0:T(8,128)(2,1)} %collective-permute-done), kind=kLoop, calls=%fused_computation.5 | loop fusion | flops 4194304 | bytes 4194304 | tf_op jit(solution)/shard_map/concatenate | solution.py:207
  34.2 0.0 copy-start.7
  34.3 0.0 copy-start.8
  34.3 0.6 collective-permute-done.1.stream_ref
  34.9 0.0 copy-start.4
  34.9 0.9 copy-done.4
  35.8 13.2 %all-to-all-done = bf16[32,8,1664]{2,1,0:T(8,128)(2,1)} async-done(((bf16[32,8,1664]{2,1,0:T(8,128)(2,1)}), bf16[32,8,1664]{2,1,0:T(8,128)(2,1)}, u32[]{:S(2)}, u32[]{:S(2)}) %all-to-all-start) | async-done | bytes 852000 | tf_op jit(solution)/shard_map/all_to_all | solution.py:197
  49.0 4.1 %collective-permute-start.2 = (bf16[256,1664]{1,0:T(8,128)(2,1)}, bf16[256,1664]{1,0:T(8,128)(2,1)}, u32[]{:S(2)}, u32[]{:S(2)}) collective-permute-start(bf16[256,1664]{1,0:T(8,128)(2,1)} %bitcast.4.refs_0_), channel_id=1, source_target_pairs={{0,8},{1,9},{2,10},{3,11},{4,12},{5,13},{6,14},{7,15},{8,16},{9,17... | collective-permute-start | bytes 2555912 | tf_op jit(solution)/shard_map/ppermute | solution.py:211
  53.0 1.9 %collective-permute-start.3 = (bf16[256,1664]{1,0:T(8,128)(2,1)}, bf16[256,1664]{1,0:T(8,128)(2,1)}, u32[]{:S(2)}, u32[]{:S(2)}) collective-permute-start(bf16[256,1664]{1,0:T(8,128)(2,1)} %bitcast.4.refs_0_), channel_id=1, source_target_pairs={{0,33},{1,34},{2,35},{3,36},{4,37},{5,38},{6,39},{7,32},{8,41},{9,... | collective-permute-start | bytes 2555912 | tf_op jit(solution)/shard_map/ppermute | solution.py:211
  55.0 7.3 %collective-permute-start.4 = (bf16[256,1664]{1,0:T(8,128)(2,1)}, bf16[256,1664]{1,0:T(8,128)(2,1)}, u32[]{:S(2)}, u32[]{:S(2)}) collective-permute-start(bf16[256,1664]{1,0:T(8,128)(2,1)} %bitcast.4.refs_0_), channel_id=1, source_target_pairs={{0,32},{1,33},{2,34},{3,35},{4,36},{5,37},{6,38},{7,39},{8,40},{9,... | collective-permute-start | bytes 2555912 | tf_op jit(solution)/shard_map/ppermute | solution.py:211
  62.3 1.9 %collective-permute-start.5 = (bf16[256,1664]{1,0:T(8,128)(2,1)}, bf16[256,1664]{1,0:T(8,128)(2,1)}, u32[]{:S(2)}, u32[]{:S(2)}) collective-permute-start(bf16[256,1664]{1,0:T(8,128)(2,1)} %bitcast.4.refs_0_), channel_id=1, source_target_pairs={{0,1},{1,2},{2,3},{3,4},{4,5},{5,6},{6,7},{7,0},{8,9},{9,10},{10,1... | collective-permute-start | bytes 2555912 | tf_op jit(solution)/shard_map/ppermute | solution.py:211
  64.2 3.4 %collective-permute-start.6 = (bf16[256,1664]{1,0:T(8,128)(2,1)}, bf16[256,1664]{1,0:T(8,128)(2,1)}, u32[]{:S(2)}, u32[]{:S(2)}) collective-permute-start(bf16[256,1664]{1,0:T(8,128)(2,1)} %bitcast.4.refs_0_), channel_id=1, source_target_pairs={{0,24},{1,25},{2,26},{3,27},{4,28},{5,29},{6,30},{7,31},{8,0},{9,1... | collective-permute-start | bytes 2555912 | tf_op jit(solution)/shard_map/ppermute | solution.py:211
  67.7 1.8 %shard_map.64.refs_5_ = f32[512,1664]{1,0:T(8,128)S(1)} custom-call(s32[1]{0:T(128)} %bitcast.13.rank_ref, bf16[8,512,256]{2,1,0:T(8,128)(2,1)S(1)} %pad_maximum_fusion.heads_ref, bf16[256,1664]{1,0:T(8,128)(2,1)} %bitcast.4.refs_0_), custom_call_target="tpu_custom_call" | custom-call | flops 436207616 | bytes 851968 | tf_op jit(solution)/shard_map/pallas_call | solution.py:130
  69.5 0.0 copy-start.1
  69.5 1.7 %copy-done.1 = f32[512,1664]{1,0:T(8,128)} copy-done((f32[512,1664]{1,0:T(8,128)}, f32[512,1664]{1,0:T(8,128)S(1)}, u32[]{:S(2)}) %copy-start.1) | copy-done | bytes 3407896
  71.2 0.0 collective-permute-done.2.refs_0_
  71.2 1.9 %collective-permute-start.7 = (bf16[256,1664]{1,0:T(8,128)(2,1)}, bf16[256,1664]{1,0:T(8,128)(2,1)}, u32[]{:S(2)}, u32[]{:S(2)}) collective-permute-start(bf16[256,1664]{1,0:T(8,128)(2,1)} %bitcast.4.refs_0_), channel_id=1, source_target_pairs={{0,416},{1,417},{2,418},{3,419},{4,420},{5,421},{6,422},{7,423},{8... | collective-permute-start | bytes 2555912 | tf_op jit(solution)/shard_map/ppermute | solution.py:214
  73.1 0.0 collective-permute-done.3.refs_1_
  73.1 3.4 %collective-permute-start.8 = (bf16[256,1664]{1,0:T(8,128)(2,1)}, bf16[256,1664]{1,0:T(8,128)(2,1)}, u32[]{:S(2)}, u32[]{:S(2)}) collective-permute-start(bf16[256,1664]{1,0:T(8,128)(2,1)} %bitcast.4.refs_0_), channel_id=1, source_target_pairs={{0,7},{1,0},{2,1},{3,2},{4,3},{5,4},{6,5},{7,6},{8,15},{9,8},{10,9... | collective-permute-start | bytes 2555912 | tf_op jit(solution)/shard_map/ppermute | solution.py:214
  76.6 0.0 copy-done.7
  76.6 0.1 dynamic_slice.18
  76.7 0.0 copy-done.8
  76.7 0.1 dynamic_slice.19
  76.8 0.1 stack.37.rank_ref
  76.9 0.1 pad_add_fusion.rank_ref
  77.0 1.2 %collective-permute-done.4.refs_2_ = bf16[256,1664]{1,0:T(8,128)(2,1)} collective-permute-done((bf16[256,1664]{1,0:T(8,128)(2,1)}, bf16[256,1664]{1,0:T(8,128)(2,1)}, u32[]{:S(2)}, u32[]{:S(2)}) %collective-permute-start.4) | collective-permute-done | bytes 852000 | tf_op jit(solution)/shard_map/ppermute | solution.py:211
  78.1 0.0 collective-permute-done.5.refs_3_
  78.1 1.3 %collective-permute-done.6.refs_4_ = bf16[256,1664]{1,0:T(8,128)(2,1)} collective-permute-done((bf16[256,1664]{1,0:T(8,128)(2,1)}, bf16[256,1664]{1,0:T(8,128)(2,1)}, u32[]{:S(2)}, u32[]{:S(2)}) %collective-permute-start.6) | collective-permute-done | bytes 852000 | tf_op jit(solution)/shard_map/ppermute | solution.py:211
  79.5 0.0 copy-start.2
  79.5 2.0 %copy-done.2 = f32[512,1664]{1,0:T(8,128)S(1)} copy-done((f32[512,1664]{1,0:T(8,128)S(1)}, f32[512,1664]{1,0:T(8,128)}, u32[]{:S(2)}) %copy-start.2) | copy-done | bytes 3407896
  81.4 0.0 copy-start.5
  81.4 5.3 %shard_map.65.so_far_ref = f32[512,1664]{1,0:T(8,128)S(1)} custom-call(s32[5]{0:T(128)S(1)} %stack.37.rank_ref, bf16[8,512,256]{2,1,0:T(8,128)(2,1)S(1)} %pad_maximum_fusion.heads_ref, bf16[256,1664]{1,0:T(8,128)(2,1)} %collective-permute-done.2.refs_0_, bf16[256,1664]{1,0:T(8,128)(2,1)} %collective-permute-done.3.refs_1_, ...), custom_call_target="tpu_custom_call" | custom-call | flops 2181038080 | bytes 4259840 | tf_op jit(solution)/shard_map/pallas_call | solution.py:130
  86.8 0.0 copy-start.3
  86.8 1.0 collective-permute-done.7.refs_0_
  87.8 2.1 %collective-permute-done.8.refs_1_ = bf16[256,1664]{1,0:T(8,128)(2,1)} collective-permute-done((bf16[256,1664]{1,0:T(8,128)(2,1)}, bf16[256,1664]{1,0:T(8,128)(2,1)}, u32[]{:S(2)}, u32[]{:S(2)}) %collective-permute-start.8) | collective-permute-done | bytes 852000 | tf_op jit(solution)/shard_map/ppermute | solution.py:214
  89.9 0.0 copy-done.5
  89.9 2.7 %shard_map.67 = bf16[256,1664]{1,0:T(8,128)(2,1)S(1)} custom-call(s32[2]{0:T(128)S(1)} %pad_add_fusion.rank_ref, bf16[8,512,256]{2,1,0:T(8,128)(2,1)S(1)} %pad_maximum_fusion.heads_ref, f32[512,1664]{1,0:T(8,128)S(1)} %shard_map.65.so_far_ref, bf16[256,1664]{1,0:T(8,128)(2,1)S(1)} %copy-done.5, f32[1,1664]{1,0:T(1,128)S(1)} %reshape.20.scale_ref, ...), custom_call_target="tpu_custom_call" | custom-call | flops 436207616 | bytes 1703936 | tf_op jit(solution)/shard_map/pallas_call | solution.py:143
  92.6 4.7 %collective-permute-start.9 = (bf16[256,1664]{1,0:T(8,128)(2,1)S(1)}, bf16[256,1664]{1,0:T(8,128)(2,1)S(1)}, u32[]{:S(2)}, u32[]{:S(2)}) collective-permute-start(bf16[256,1664]{1,0:T(8,128)(2,1)S(1)} %shard_map.67), channel_id=1, source_target_pairs={{0,64},{1,65},{2,66},{3,67},{4,68},{5,69},{6,70},{7,71},{8,72},{9,... | collective-permute-start | bytes 2555912 | tf_op jit(solution)/shard_map/ppermute | solution.py:218
  97.4 0.0 copy-done.3
  97.4 2.7 %shard_map.66.own_ref = bf16[256,1664]{1,0:T(8,128)(2,1)S(1)} custom-call(s32[2]{0:T(128)S(1)} %pad_add_fusion.rank_ref, bf16[8,512,256]{2,1,0:T(8,128)(2,1)S(1)} %pad_maximum_fusion.heads_ref, f32[512,1664]{1,0:T(8,128)S(1)} %shard_map.65.so_far_ref, bf16[256,1664]{1,0:T(8,128)(2,1)S(1)} %copy-done.3, f32[1,1664]{1,0:T(1,128)S(1)} %reshape.20.scale_ref, ...), custom_call_target="tpu_custom_call" | custom-call | flops 436207616 | bytes 1703936 | tf_op jit(solution)/shard_map/pallas_call | solution.py:143
  100.1 0.0 collective-permute-done.9.other_ref
  100.1 1.3 %shard_map.68 = bf16[256,3200]{1,0:T(8,128)(2,1)} custom-call(s32[1]{0:T(128)} %bitcast.core_ref, bf16[256,1664]{1,0:T(8,128)(2,1)S(1)} %shard_map.66.own_ref, bf16[256,1664]{1,0:T(8,128)(2,1)S(1)} %collective-permute-done.9.other_ref), custom_call_target="tpu_custom_call" | custom-call | tf_op jit(solution)/shard_map/pallas_call | solution.py:168
  (4 shorter events, 0.0 us)
Async XLA Ops:
  0.0 21.8 %copy-start = (bf16[256,2048]{1,0:T(8,128)(2,1)S(1)}, bf16[256,2048]{1,0:T(8,128)(2,1)}, u32[]{:S(2)}) copy-start(bf16[256,2048]{1,0:T(8,128)(2,1)} %param.7) | copy-start | bytes 3145732
  9.7 39.2 %all-to-all-start = ((bf16[32,8,1664]{2,1,0:T(8,128)(2,1)}), bf16[32,8,1664]{2,1,0:T(8,128)(2,1)}, u32[]{:S(2)}, u32[]{:S(2)}) async-start(bf16[32,8,1664]{2,1,0:T(8,128)(2,1)} %broadcast_in_dim.8), calls=%async_computation | async-start | bytes 1703936 | tf_op jit(solution)/shard_map/all_to_all | solution.py:197
  25.6 6.9 %copy-start.6 = (bf16[256,8,256]{2,0,1:T(8,128)(2,1)}, bf16[256,8,256]{2,0,1:T(8,128)(2,1)S(1)}, u32[]{:S(2)}) copy-start(bf16[256,8,256]{2,0,1:T(8,128)(2,1)S(1)} %copy.8) | copy-start | bytes 3145732
  25.6 6.9 %collective-permute-start = (bf16[8,256,256]{2,1,0:T(8,128)(2,1)S(1)}, bf16[8,256,256]{2,1,0:T(8,128)(2,1)}, u32[]{:S(2)}, u32[]{:S(2)}) collective-permute-start(bf16[8,256,256]{2,1,0:T(8,128)(2,1)S(1)} %bitcast.16), channel_id=1, source_target_pairs={{0,64},{1,65},{2,66},{3,67},{4,68},{5,69},{6,70},{7,71},{8,72},{9,... | collective-permute-start | bytes 3145736 | tf_op jit(solution)/shard_map/ppermute | solution.py:202
  30.6 4.3 %collective-permute-start.1 = (bf16[256,1664]{1,0:T(8,128)(2,1)S(1)}, bf16[256,1664]{1,0:T(8,128)(2,1)S(1)}, u32[]{:S(2)}, u32[]{:S(2)}) collective-permute-start(bf16[256,1664]{1,0:T(8,128)(2,1)S(1)} %get-tuple-element.17), channel_id=1, source_target_pairs={{0,64},{1,65},{2,66},{3,67},{4,68},{5,69},{6,70},{7,71},{8,72},{9,... | collective-permute-start | bytes 2555912 | tf_op jit(solution)/shard_map/ppermute | solution.py:204
  34.2 42.4 %copy-start.7 = (f32[3200]{0:T(1024)S(1)}, f32[3200]{0:T(1024)}, u32[]{:S(2)}) copy-start(f32[3200]{0:T(1024)} %param.10) | copy-start | bytes 38404
  34.3 42.5 %copy-start.8 = (f32[3200]{0:T(1024)S(1)}, f32[3200]{0:T(1024)}, u32[]{:S(2)}) copy-start(f32[3200]{0:T(1024)} %param.9) | copy-start | bytes 38404
  34.9 0.9 copy-start.4
  49.0 22.2 %collective-permute-start.2 = (bf16[256,1664]{1,0:T(8,128)(2,1)}, bf16[256,1664]{1,0:T(8,128)(2,1)}, u32[]{:S(2)}, u32[]{:S(2)}) collective-permute-start(bf16[256,1664]{1,0:T(8,128)(2,1)} %bitcast.4.refs_0_), channel_id=1, source_target_pairs={{0,8},{1,9},{2,10},{3,11},{4,12},{5,13},{6,14},{7,15},{8,16},{9,17... | collective-permute-start | bytes 2555912 | tf_op jit(solution)/shard_map/ppermute | solution.py:211
  53.0 20.1 %collective-permute-start.3 = (bf16[256,1664]{1,0:T(8,128)(2,1)}, bf16[256,1664]{1,0:T(8,128)(2,1)}, u32[]{:S(2)}, u32[]{:S(2)}) collective-permute-start(bf16[256,1664]{1,0:T(8,128)(2,1)} %bitcast.4.refs_0_), channel_id=1, source_target_pairs={{0,33},{1,34},{2,35},{3,36},{4,37},{5,38},{6,39},{7,32},{8,41},{9,... | collective-permute-start | bytes 2555912 | tf_op jit(solution)/shard_map/ppermute | solution.py:211
  55.0 23.2 %collective-permute-start.4 = (bf16[256,1664]{1,0:T(8,128)(2,1)}, bf16[256,1664]{1,0:T(8,128)(2,1)}, u32[]{:S(2)}, u32[]{:S(2)}) collective-permute-start(bf16[256,1664]{1,0:T(8,128)(2,1)} %bitcast.4.refs_0_), channel_id=1, source_target_pairs={{0,32},{1,33},{2,34},{3,35},{4,36},{5,37},{6,38},{7,39},{8,40},{9,... | collective-permute-start | bytes 2555912 | tf_op jit(solution)/shard_map/ppermute | solution.py:211
  62.3 15.9 %collective-permute-start.5 = (bf16[256,1664]{1,0:T(8,128)(2,1)}, bf16[256,1664]{1,0:T(8,128)(2,1)}, u32[]{:S(2)}, u32[]{:S(2)}) collective-permute-start(bf16[256,1664]{1,0:T(8,128)(2,1)} %bitcast.4.refs_0_), channel_id=1, source_target_pairs={{0,1},{1,2},{2,3},{3,4},{4,5},{5,6},{6,7},{7,0},{8,9},{9,10},{10,1... | collective-permute-start | bytes 2555912 | tf_op jit(solution)/shard_map/ppermute | solution.py:211
  64.2 15.3 %collective-permute-start.6 = (bf16[256,1664]{1,0:T(8,128)(2,1)}, bf16[256,1664]{1,0:T(8,128)(2,1)}, u32[]{:S(2)}, u32[]{:S(2)}) collective-permute-start(bf16[256,1664]{1,0:T(8,128)(2,1)} %bitcast.4.refs_0_), channel_id=1, source_target_pairs={{0,24},{1,25},{2,26},{3,27},{4,28},{5,29},{6,30},{7,31},{8,0},{9,1... | collective-permute-start | bytes 2555912 | tf_op jit(solution)/shard_map/ppermute | solution.py:211
  69.5 1.7 %copy-start.1 = (f32[512,1664]{1,0:T(8,128)}, f32[512,1664]{1,0:T(8,128)S(1)}, u32[]{:S(2)}) copy-start(f32[512,1664]{1,0:T(8,128)S(1)} %shard_map.64.refs_5_) | copy-start | bytes 10223620
  71.2 16.6 %collective-permute-start.7 = (bf16[256,1664]{1,0:T(8,128)(2,1)}, bf16[256,1664]{1,0:T(8,128)(2,1)}, u32[]{:S(2)}, u32[]{:S(2)}) collective-permute-start(bf16[256,1664]{1,0:T(8,128)(2,1)} %bitcast.4.refs_0_), channel_id=1, source_target_pairs={{0,416},{1,417},{2,418},{3,419},{4,420},{5,421},{6,422},{7,423},{8... | collective-permute-start | bytes 2555912 | tf_op jit(solution)/shard_map/ppermute | solution.py:214
  73.1 16.8 %collective-permute-start.8 = (bf16[256,1664]{1,0:T(8,128)(2,1)}, bf16[256,1664]{1,0:T(8,128)(2,1)}, u32[]{:S(2)}, u32[]{:S(2)}) collective-permute-start(bf16[256,1664]{1,0:T(8,128)(2,1)} %bitcast.4.refs_0_), channel_id=1, source_target_pairs={{0,7},{1,0},{2,1},{3,2},{4,3},{5,4},{6,5},{7,6},{8,15},{9,8},{10,9... | collective-permute-start | bytes 2555912 | tf_op jit(solution)/shard_map/ppermute | solution.py:214
  79.5 2.0 %copy-start.2 = (f32[512,1664]{1,0:T(8,128)S(1)}, f32[512,1664]{1,0:T(8,128)}, u32[]{:S(2)}) copy-start(f32[512,1664]{1,0:T(8,128)} %copy-done.1) | copy-start | bytes 10223620
  81.4 8.5 %copy-start.5 = (bf16[256,1664]{1,0:T(8,128)(2,1)S(1)}, bf16[256,1664]{1,0:T(8,128)(2,1)}, u32[]{:S(2)}) copy-start(bf16[256,1664]{1,0:T(8,128)(2,1)} %copy-done.4) | copy-start | bytes 2555908
  86.8 10.6 %copy-start.3 = (bf16[256,1664]{1,0:T(8,128)(2,1)S(1)}, bf16[256,1664]{1,0:T(8,128)(2,1)}, u32[]{:S(2)}) copy-start(bf16[256,1664]{1,0:T(8,128)(2,1)} %get-tuple-element.14.stream_ref) | copy-start | bytes 2555908
  92.6 7.5 %collective-permute-start.9 = (bf16[256,1664]{1,0:T(8,128)(2,1)S(1)}, bf16[256,1664]{1,0:T(8,128)(2,1)S(1)}, u32[]{:S(2)}, u32[]{:S(2)}) collective-permute-start(bf16[256,1664]{1,0:T(8,128)(2,1)S(1)} %shard_map.67), channel_id=1, source_target_pairs={{0,64},{1,65},{2,66},{3,67},{4,68},{5,69},{6,70},{7,71},{8,72},{9,... | collective-permute-start | bytes 2555912 | tf_op jit(solution)/shard_map/ppermute | solution.py:218

commit v4 on v3

--- a/solution.py
+++ b/solution.py
@@ -68,13 +68,13 @@
     np.int32,
 )
 STEPS = [
+    ((0, 1, 1), (0, -1, -1)),
     ((1, 0, 0), (-1, 0, 0)),
-    ((0, 1, 1), (0, -1, -1)),
     ((0, 1, 0), (0, -1, 0)),
     ((0, 0, 1), (0, 0, -1)),
-    ((-1, 0, 0), (1, 0, 0)),
     ((0, -1, 0), (0, 1, 0)),
     ((0, 0, -1), (0, 0, 1)),
+    ((-1, 0, 0), (1, 0, 0)),
 ]
 
 def fetch(block_refs, slots, sems):
@@ -84,17 +84,27 @@
     return copies
 
 
+def own_kernel(rank_ref, heads_ref, block_ref, total_ref, slots, sems):
+    fetch([block_ref], slots, sems)[0].wait()
+    for columns in TILES:
+        total_ref[:, columns] = jnp.dot(
+            heads_ref[rank_ref[0], :TOK], slots[0, :, columns], preferred_element_type=jnp.float32
+        )
+
+
 def early_kernel(n, rank_ref, heads_ref, *refs):
-    block_refs, so_far_ref, (total_ref, slots, sems) = refs[:n], refs[n:-3], refs[-3:]
+    block_refs, (so_far_ref, total_ref, slots, sems) = refs[:n], refs[n:]
     copies = fetch(block_refs, slots, sems)
     for copy in copies:
         copy.wait()
     for columns in TILES:
-        total = so_far_ref[0][:, columns] if so_far_ref else 0.0
-        for k in range(n):
+        total = 0.0
+        for k in range(1, n):
             part = slots[k, :, columns]
             total = total + jnp.dot(heads_ref[rank_ref[k]], part, preferred_element_type=jnp.float32)
-        total_ref[:, columns] = total
+        own = jnp.dot(heads_ref[rank_ref[0], TOK:], slots[0, :, columns], preferred_element_type=jnp.float32)
+        total_ref[:TOK, columns] = total[:TOK] + so_far_ref[:, columns]
+        total_ref[TOK:, columns] = total[TOK:] + own
 
 
 def late_kernel(rows, rank_ref, heads_ref, so_far_ref, stream_ref, scale_ref, bias_ref, *refs):
@@ -125,17 +135,29 @@
     return pl.CostEstimate(flops=2 * rows * n * DEPTH * WIDE, bytes_accessed=n * DEPTH * WIDE * 2, transcendentals=0)
 
 
-def early(ranks, heads, blocks, *so_far):
+def own_sum(ranks, heads, block):
+    return pl.pallas_call(
+        own_kernel,
+        in_specs=[SMEM_SPEC, VMEM_SPEC, ANY_SPEC],
+        out_specs=VMEM_SPEC,
+        out_shape=jax.ShapeDtypeStruct((TOK, WIDE), jnp.float32),
+        scratch_shapes=slots_for(1),
+        compiler_params=pltpu.CompilerParams(vmem_limit_bytes=24 * MIB),
+        cost_estimate=cost(1, TOK),
+    )(ranks, heads, block)
+
+
+def early(ranks, heads, blocks, so_far):
     n = len(blocks)
     return pl.pallas_call(
         functools.partial(early_kernel, n),
-        in_specs=[SMEM_SPEC, VMEM_SPEC] + [ANY_SPEC] * n + [VMEM_SPEC] * len(so_far),
+        in_specs=[SMEM_SPEC, VMEM_SPEC] + [ANY_SPEC] * n + [VMEM_SPEC],
         out_specs=VMEM_SPEC,
         out_shape=jax.ShapeDtypeStruct((2 * TOK, WIDE), jnp.float32),
         scratch_shapes=slots_for(n),
         compiler_params=pltpu.CompilerParams(vmem_limit_bytes=24 * MIB),
         cost_estimate=cost(n, 2 * TOK),
-    )(ranks, heads, *blocks, *so_far)
+    )(ranks, heads, *blocks, so_far)
 
 
 def late(half, ranks, heads, so_far, stream, scale, bias, blocks):
@@ -209,10 +231,10 @@
 
     ranks = jnp.stack([mine] + [(mine - rise(core, *step)) % CLASSES for step in STEPS]).astype(jnp.int32)
     blocks = [block] + [lax.ppermute(block, "d", moves(*step)) for step in STEPS[:AHEAD]]
-    total = early(ranks[:FIRST], heads, blocks[:FIRST])
+    total = own_sum(ranks[:1], heads, block)
     block, total = lax.optimization_barrier((block, total))
     blocks += [lax.ppermute(block, "d", moves(*step)) for step in STEPS[AHEAD:]]
-    total = early(ranks[FIRST:SOON], heads, blocks[FIRST:SOON], total)
+    total = early(ranks[:SOON], heads, blocks[:SOON], total)
     last = (ranks[SOON:], heads, total)
     other = late(0, *last, other_stream, scale, bias, blocks[SOON:])
     came = lax.ppermute(other, "d", OTHER_CORE)
@@ -220,7 +242,6 @@
     return join(core, own, came)
 
 
-FIRST = 1
 AHEAD = 5
 SOON = 6
 

time: 102 us -> 102 us (level)
  waiting for transfers between devices: 19.4 us -> 22.4 us
  starting transfers between devices: 45.1 us -> 42.3 us
  local copies, waits for them, and re-layouts: 8.85 us -> 7.82 us
    ppermute x5, waiting for transfers between devices: 2.5 us -> 8.65 us  [body(): lax.ppermute(block, 'd', moves(*step))]
    ppermute x2, waiting for transfers between devices: 3.1 us -> 0.01 us  [body(): blocks += [lax.ppermute(block, 'd', moves(*step)) for step in STEPS[AHEAD:]]]
    ppermute x1, starting transfers between devices: 4.75 us -> 1.92 us  [body(): came = lax.ppermute(other, 'd', OTHER_CORE)]
    pallas_call x0 -> x1, Pallas kernels: none -> 1.58 us  [own_sum(): pl.pallas_call(own_kernel, in_specs=[SMEM_SPEC, VMEM_SPEC, ANY_SPEC], out...]
    ppermute x5, starting transfers between devices: 18.6 us -> 17.2 us  [body(): lax.ppermute(block, 'd', moves(*step))]
    ppermute x2, starting transfers between devices: 5.27 us -> 6.72 us  [body(): blocks += [lax.ppermute(block, 'd', moves(*step)) for step in STEPS[AHEAD:]]]
    pallas_call x2 -> x1, Pallas kernels: 7.16 us -> 5.84 us  [early(): pl.pallas_call(functools.partial(early_kernel, n), in_specs=[SMEM_SPEC, V...]
  transfers between devices with their start and end apart: 11 -> 11, of which waited for: 6 -> 4; matrix products, arithmetic and copies ran while one was open for 8% -> 8% of each run, Pallas kernels for 10% -> 10%
where the time goes in v4:
time: 102 us; the launch traced here: 101 us
  starting transfers between devices  42.3 us (41%)
  waiting for transfers between devices  22.4 us (22%)
  Pallas kernels  14.1 us (14%)
  blocking collectives  8.71 us (9%)
  local copies, waits for them, and re-layouts  7.82 us (8%)
  matrix products  3.25 us (3%)
  other arithmetic  1.76 us (2%)
    ppermute x5, starting transfers between devices, body(): lax.ppermute(block, 'd', moves(*step))  17.2 us
    all_to_all x1, waiting for transfers between devices, body(): lax.all_to_all(for_each, 'd', 0, 0, axis_index_groups=GROUPS, tiled=True)  13.2 us
    all_to_all x1, starting transfers between devices, body(): lax.all_to_all(for_each, 'd', 0, 0, axis_index_groups=GROUPS, tiled=True)  12.1 us
    all_gather x1, blocking collectives, body(): lax.all_gather(out_weight, 'd', axis=0, axis_index_groups=CHIP_PAIRS)  8.71 us
    ppermute x5, waiting for transfers between devices, body(): lax.ppermute(block, 'd', moves(*step))  8.65 us
    ppermute x2, starting transfers between devices, body(): blocks += [lax.ppermute(block, 'd', moves(*step)) for step in STEPS[AHEAD:]]  6.72 us
    pallas_call x1, Pallas kernels, early(): pl.pallas_call(functools.partial(early_kernel, n), in_specs=[SMEM_SPEC, V...  5.84 us
    pallas_call x2, Pallas kernels, late(): pl.pallas_call(functools.partial(late_kernel, slice(half * TOK, (half + 1...  5.37 us
  transfers between devices with their start and end apart: 11, of which 4 were waited for; matrix products, arithmetic and copies ran while one was open for 8% of the time, Pallas kernels for 10%

profile of v4, /device:TPU:1, one launch (start us, length us, event | category | flops | bytes accessed | tf_op | source)
XLA Modules:
  0.0 100.8 jit_solution(15467919470045067793)
XLA Ops:
  0.0 0.0 copy-start
  0.0 8.7 %all-gather.1 = bf16[2,4,3200]{2,1,0:T(4,128)(2,1)S(1)} all-gather(bf16[1,4,3200]{2,1,0:T(4,128)(2,1)} %bitcast.19), channel_id=2, replica_groups={{0,64},{1,65},{2,66},{3,67},{4,68},{5,69},{6,70},{7,71},{8,72},{9,73},{..., dimensions={0}, use_global_device_ids=true | all-gather | bytes 76800 | tf_op jit(solution)/shard_map/all_gather | solution.py:216
  8.7 1.0 broadcast_in_dim.8
  9.7 12.1 %all-to-all-start = ((bf16[32,8,1664]{2,1,0:T(8,128)(2,1)}), bf16[32,8,1664]{2,1,0:T(8,128)(2,1)}, u32[]{:S(2)}, u32[]{:S(2)}) async-start(bf16[32,8,1664]{2,1,0:T(8,128)(2,1)} %broadcast_in_dim.8), calls=%async_computation | async-start | bytes 1703936 | tf_op jit(solution)/shard_map/all_to_all | solution.py:219
  21.8 0.0 copy-done
  21.8 3.2 %fusion.4 = bf16[2048,256]{1,0:T(8,128)(2,1)S(1)} fusion(bf16[256,2048]{1,0:T(8,128)(2,1)S(1)} %copy-done, s32[2048]{0:T(1024)} %constant.141), kind=kOutput, calls=%fused_computation.4 | convolution fusion | flops 2156396544 | bytes 2105344 | tf_op jit(solution)/shard_map/dot_general | solution.py:222
  25.1 0.5 copy.8
  25.6 0.0 copy-start.6
  25.6 2.5 %collective-permute-start = (bf16[8,256,256]{2,1,0:T(8,128)(2,1)S(1)}, bf16[8,256,256]{2,1,0:T(8,128)(2,1)}, u32[]{:S(2)}, u32[]{:S(2)}) collective-permute-start(bf16[8,256,256]{2,1,0:T(8,128)(2,1)S(1)} %bitcast.16), channel_id=1, source_target_pairs={{0,64},{1,65},{2,66},{3,67},{4,68},{5,69},{6,70},{7,71},{8,72},{9,... | collective-permute-start | bytes 3145736 | tf_op jit(solution)/shard_map/ppermute | solution.py:224
  28.2 2.4 %constant_dynamic-slice_fusion = (bf16[256,1664]{1,0:T(8,128)(2,1)S(1)}, bf16[256,1664]{1,0:T(8,128)(2,1)}) fusion(bf16[256,3200]{1,0:T(8,128)(2,1)} %param.6, s32[]{:T(128)S(6)} %select_n.85, s32[]{:T(128)S(6)} %select_n.84), kind=kLoop, calls=%fused_computation.6 | loop fusion | bytes 3407880 | tf_op jit(solution)/shard_map/dynamic_slice | solution.py:226
  30.6 1.9 %collective-permute-start.1 = (bf16[256,1664]{1,0:T(8,128)(2,1)S(1)}, bf16[256,1664]{1,0:T(8,128)(2,1)S(1)}, u32[]{:S(2)}, u32[]{:S(2)}) collective-permute-start(bf16[256,1664]{1,0:T(8,128)(2,1)S(1)} %get-tuple-element.17), channel_id=1, source_target_pairs={{0,64},{1,65},{2,66},{3,67},{4,68},{5,69},{6,70},{7,71},{8,72},{9,... | collective-permute-start | bytes 2555912 | tf_op jit(solution)/shard_map/ppermute | solution.py:226
  32.5 0.0 copy-done.6
  32.5 0.0 collective-permute-done
  32.5 1.7 %pad_maximum_fusion.heads_ref = bf16[8,512,256]{2,1,0:T(8,128)(2,1)S(1)} fusion(bf16[8,256,256]{2,1,0:T(8,128)(2,1)} %bitcast.17, bf16[8,256,256]{2,1,0:T(8,128)(2,1)} %collective-permute-done), kind=kLoop, calls=%fused_computation.5 | loop fusion | flops 4194304 | bytes 4194304 | tf_op jit(solution)/shard_map/concatenate | solution.py:229
  34.2 0.0 copy-start.7
  34.2 0.0 copy-start.8
  34.2 0.6 collective-permute-done.1.stream_ref
  34.9 0.0 copy-start.4
  34.9 0.9 copy-done.4
  35.8 13.2 %all-to-all-done = bf16[32,8,1664]{2,1,0:T(8,128)(2,1)} async-done(((bf16[32,8,1664]{2,1,0:T(8,128)(2,1)}), bf16[32,8,1664]{2,1,0:T(8,128)(2,1)}, u32[]{:S(2)}, u32[]{:S(2)}) %all-to-all-start) | async-done | bytes 852000 | tf_op jit(solution)/shard_map/all_to_all | solution.py:219
  48.9 1.9 %collective-permute-start.2 = (bf16[256,1664]{1,0:T(8,128)(2,1)}, bf16[256,1664]{1,0:T(8,128)(2,1)}, u32[]{:S(2)}, u32[]{:S(2)}) collective-permute-start(bf16[256,1664]{1,0:T(8,128)(2,1)} %bitcast.4.block_ref.refs_0_), channel_id=1, source_target_pairs={{0,33},{1,34},{2,35},{3,36},{4,37},{5,38},{6,39},{7,32},{8,41},{9,... | collective-permute-start | bytes 2555912 | tf_op jit(solution)/shard_map/ppermute | solution.py:233
  50.8 4.1 %collective-permute-start.3 = (bf16[256,1664]{1,0:T(8,128)(2,1)}, bf16[256,1664]{1,0:T(8,128)(2,1)}, u32[]{:S(2)}, u32[]{:S(2)}) collective-permute-start(bf16[256,1664]{1,0:T(8,128)(2,1)} %bitcast.4.block_ref.refs_0_), channel_id=1, source_target_pairs={{0,8},{1,9},{2,10},{3,11},{4,12},{5,13},{6,14},{7,15},{8,16},{9,17... | collective-permute-start | bytes 2555912 | tf_op jit(solution)/shard_map/ppermute | solution.py:233
  54.9 7.3 %collective-permute-start.4 = (bf16[256,1664]{1,0:T(8,128)(2,1)}, bf16[256,1664]{1,0:T(8,128)(2,1)}, u32[]{:S(2)}, u32[]{:S(2)}) collective-permute-start(bf16[256,1664]{1,0:T(8,128)(2,1)} %bitcast.4.block_ref.refs_0_), channel_id=1, source_target_pairs={{0,32},{1,33},{2,34},{3,35},{4,36},{5,37},{6,38},{7,39},{8,40},{9,... | collective-permute-start | bytes 2555912 | tf_op jit(solution)/shard_map/ppermute | solution.py:233
  62.3 1.9 %collective-permute-start.5 = (bf16[256,1664]{1,0:T(8,128)(2,1)}, bf16[256,1664]{1,0:T(8,128)(2,1)}, u32[]{:S(2)}, u32[]{:S(2)}) collective-permute-start(bf16[256,1664]{1,0:T(8,128)(2,1)} %bitcast.4.block_ref.refs_0_), channel_id=1, source_target_pairs={{0,1},{1,2},{2,3},{3,4},{4,5},{5,6},{6,7},{7,0},{8,9},{9,10},{10,1... | collective-permute-start | bytes 2555912 | tf_op jit(solution)/shard_map/ppermute | solution.py:233
  64.2 1.9 %collective-permute-start.6 = (bf16[256,1664]{1,0:T(8,128)(2,1)}, bf16[256,1664]{1,0:T(8,128)(2,1)}, u32[]{:S(2)}, u32[]{:S(2)}) collective-permute-start(bf16[256,1664]{1,0:T(8,128)(2,1)} %bitcast.4.block_ref.refs_0_), channel_id=1, source_target_pairs={{0,416},{1,417},{2,418},{3,419},{4,420},{5,421},{6,422},{7,423},{8... | collective-permute-start | bytes 2555912 | tf_op jit(solution)/shard_map/ppermute | solution.py:233
  66.2 1.6 %shard_map.64.refs_6_ = f32[256,1664]{1,0:T(8,128)S(1)} custom-call(s32[1]{0:T(128)} %bitcast.8.rank_ref, bf16[8,512,256]{2,1,0:T(8,128)(2,1)S(1)} %pad_maximum_fusion.heads_ref, bf16[256,1664]{1,0:T(8,128)(2,1)} %bitcast.4.block_ref.refs_0_), custom_call_target="tpu_custom_call" | custom-call | flops 218103808 | bytes 851968 | tf_op jit(solution)/shard_map/pallas_call | solution.py:139
  67.8 0.0 copy-start.1
  67.8 1.2 %copy-done.1 = f32[256,1664]{1,0:T(8,128)} copy-done((f32[256,1664]{1,0:T(8,128)}, f32[256,1664]{1,0:T(8,128)S(1)}, u32[]{:S(2)}) %copy-start.1) | copy-done | bytes 1703960
  69.0 0.0 collective-permute-done.2.refs_1_
  69.0 3.4 %collective-permute-start.7 = (bf16[256,1664]{1,0:T(8,128)(2,1)}, bf16[256,1664]{1,0:T(8,128)(2,1)}, u32[]{:S(2)}, u32[]{:S(2)}) collective-permute-start(bf16[256,1664]{1,0:T(8,128)(2,1)} %bitcast.4.block_ref.refs_0_), channel_id=1, source_target_pairs={{0,7},{1,0},{2,1},{3,2},{4,3},{5,4},{6,5},{7,6},{8,15},{9,8},{10,9... | collective-permute-start | bytes 2555912 | tf_op jit(solution)/shard_map/ppermute | solution.py:236
  72.4 0.0 collective-permute-done.3.refs_2_
  72.4 3.4 %collective-permute-start.8 = (bf16[256,1664]{1,0:T(8,128)(2,1)}, bf16[256,1664]{1,0:T(8,128)(2,1)}, u32[]{:S(2)}, u32[]{:S(2)}) collective-permute-start(bf16[256,1664]{1,0:T(8,128)(2,1)} %bitcast.4.block_ref.refs_0_), channel_id=1, source_target_pairs={{0,24},{1,25},{2,26},{3,27},{4,28},{5,29},{6,30},{7,31},{8,0},{9,1... | collective-permute-start | bytes 2555912 | tf_op jit(solution)/shard_map/ppermute | solution.py:236
  75.9 0.0 copy-done.7
  75.9 0.1 dynamic_slice.18
  76.0 0.0 copy-done.8
  76.0 0.1 dynamic_slice.19
  76.1 0.1 stack.38.rank_ref
  76.2 0.1 pad_add_fusion.rank_ref
  76.2 1.0 collective-permute-done.4.refs_3_
  77.2 0.0 collective-permute-done.5.refs_4_
  77.2 7.7 %collective-permute-done.6.refs_5_ = bf16[256,1664]{1,0:T(8,128)(2,1)} collective-permute-done((bf16[256,1664]{1,0:T(8,128)(2,1)}, bf16[256,1664]{1,0:T(8,128)(2,1)}, u32[]{:S(2)}, u32[]{:S(2)}) %collective-permute-start.6) | collective-permute-done | bytes 852000 | tf_op jit(solution)/shard_map/ppermute | solution.py:233
  84.9 0.0 copy-start.2
  84.9 1.5 %copy-done.2 = f32[256,1664]{1,0:T(8,128)S(1)} copy-done((f32[256,1664]{1,0:T(8,128)S(1)}, f32[256,1664]{1,0:T(8,128)}, u32[]{:S(2)}) %copy-start.2) | copy-done | bytes 1703960
  86.3 0.0 copy-start.5
  86.3 5.8 %shard_map.65.so_far_ref = f32[512,1664]{1,0:T(8,128)S(1)} custom-call(s32[6]{0:T(128)S(1)} %stack.38.rank_ref, bf16[8,512,256]{2,1,0:T(8,128)(2,1)S(1)} %pad_maximum_fusion.heads_ref, bf16[256,1664]{1,0:T(8,128)(2,1)} %bitcast.4.block_ref.refs_0_, bf16[256,1664]{1,0:T(8,128)(2,1)} %collective-permute-done.2.refs_1_, ...), custom_call_target="tpu_custom_call" | custom-call | flops 2617245696 | bytes 5111808 | tf_op jit(solution)/shard_map/pallas_call | solution.py:152
  92.2 0.0 copy-start.3
  92.2 0.0 collective-permute-done.7.refs_0_
  92.2 0.0 collective-permute-done.8.refs_1_
  92.2 0.0 copy-done.5
  92.2 2.7 %shard_map.67 = bf16[256,1664]{1,0:T(8,128)(2,1)S(1)} custom-call(s32[2]{0:T(128)S(1)} %pad_add_fusion.rank_ref, bf16[8,512,256]{2,1,0:T(8,128)(2,1)S(1)} %pad_maximum_fusion.heads_ref, f32[512,1664]{1,0:T(8,128)S(1)} %shard_map.65.so_far_ref, bf16[256,1664]{1,0:T(8,128)(2,1)S(1)} %copy-done.5, f32[1,1664]{1,0:T(1,128)S(1)} %reshape.20.scale_ref, ...), custom_call_target="tpu_custom_call" | custom-call | flops 436207616 | bytes 1703936 | tf_op jit(solution)/shard_map/pallas_call | solution.py:165
  94.9 1.9 %collective-permute-start.9 = (bf16[256,1664]{1,0:T(8,128)(2,1)S(1)}, bf16[256,1664]{1,0:T(8,128)(2,1)S(1)}, u32[]{:S(2)}, u32[]{:S(2)}) collective-permute-start(bf16[256,1664]{1,0:T(8,128)(2,1)S(1)} %shard_map.67), channel_id=1, source_target_pairs={{0,64},{1,65},{2,66},{3,67},{4,68},{5,69},{6,70},{7,71},{8,72},{9,... | collective-permute-start | bytes 2555912 | tf_op jit(solution)/shard_map/ppermute | solution.py:240
  96.9 0.0 copy-done.3
  96.9 2.7 %shard_map.66.own_ref = bf16[256,1664]{1,0:T(8,128)(2,1)S(1)} custom-call(s32[2]{0:T(128)S(1)} %pad_add_fusion.rank_ref, bf16[8,512,256]{2,1,0:T(8,128)(2,1)S(1)} %pad_maximum_fusion.heads_ref, f32[512,1664]{1,0:T(8,128)S(1)} %shard_map.65.so_far_ref, bf16[256,1664]{1,0:T(8,128)(2,1)S(1)} %copy-done.3, f32[1,1664]{1,0:T(1,128)S(1)} %reshape.20.scale_ref, ...), custom_call_target="tpu_custom_call" | custom-call | flops 436207616 | bytes 1703936 | tf_op jit(solution)/shard_map/pallas_call | solution.py:165
  99.6 0.0 collective-permute-done.9.other_ref
  99.6 1.3 %shard_map.68 = bf16[256,3200]{1,0:T(8,128)(2,1)} custom-call(s32[1]{0:T(128)} %bitcast.core_ref, bf16[256,1664]{1,0:T(8,128)(2,1)S(1)} %shard_map.66.own_ref, bf16[256,1664]{1,0:T(8,128)(2,1)S(1)} %collective-permute-done.9.other_ref), custom_call_target="tpu_custom_call" | custom-call | tf_op jit(solution)/shard_map/pallas_call | solution.py:190
  (4 shorter events, 0.0 us)
Async XLA Ops:
  0.0 21.8 %copy-start = (bf16[256,2048]{1,0:T(8,128)(2,1)S(1)}, bf16[256,2048]{1,0:T(8,128)(2,1)}, u32[]{:S(2)}) copy-start(bf16[256,2048]{1,0:T(8,128)(2,1)} %param.7) | copy-start | bytes 3145732
  9.7 39.2 %all-to-all-start = ((bf16[32,8,1664]{2,1,0:T(8,128)(2,1)}), bf16[32,8,1664]{2,1,0:T(8,128)(2,1)}, u32[]{:S(2)}, u32[]{:S(2)}) async-start(bf16[32,8,1664]{2,1,0:T(8,128)(2,1)} %broadcast_in_dim.8), calls=%async_computation | async-start | bytes 1703936 | tf_op jit(solution)/shard_map/all_to_all | solution.py:219
  25.6 6.9 %copy-start.6 = (bf16[256,8,256]{2,0,1:T(8,128)(2,1)}, bf16[256,8,256]{2,0,1:T(8,128)(2,1)S(1)}, u32[]{:S(2)}) copy-start(bf16[256,8,256]{2,0,1:T(8,128)(2,1)S(1)} %copy.8) | copy-start | bytes 3145732
  25.6 6.9 %collective-permute-start = (bf16[8,256,256]{2,1,0:T(8,128)(2,1)S(1)}, bf16[8,256,256]{2,1,0:T(8,128)(2,1)}, u32[]{:S(2)}, u32[]{:S(2)}) collective-permute-start(bf16[8,256,256]{2,1,0:T(8,128)(2,1)S(1)} %bitcast.16), channel_id=1, source_target_pairs={{0,64},{1,65},{2,66},{3,67},{4,68},{5,69},{6,70},{7,71},{8,72},{9,... | collective-permute-start | bytes 3145736 | tf_op jit(solution)/shard_map/ppermute | solution.py:224
  30.6 4.3 %collective-permute-start.1 = (bf16[256,1664]{1,0:T(8,128)(2,1)S(1)}, bf16[256,1664]{1,0:T(8,128)(2,1)S(1)}, u32[]{:S(2)}, u32[]{:S(2)}) collective-permute-start(bf16[256,1664]{1,0:T(8,128)(2,1)S(1)} %get-tuple-element.17), channel_id=1, source_target_pairs={{0,64},{1,65},{2,66},{3,67},{4,68},{5,69},{6,70},{7,71},{8,72},{9,... | collective-permute-start | bytes 2555912 | tf_op jit(solution)/shard_map/ppermute | solution.py:226
  34.2 41.7 %copy-start.7 = (f32[3200]{0:T(1024)S(1)}, f32[3200]{0:T(1024)}, u32[]{:S(2)}) copy-start(f32[3200]{0:T(1024)} %param.10) | copy-start | bytes 38404
  34.2 41.7 %copy-start.8 = (f32[3200]{0:T(1024)S(1)}, f32[3200]{0:T(1024)}, u32[]{:S(2)}) copy-start(f32[3200]{0:T(1024)} %param.9) | copy-start | bytes 38404
  34.9 0.9 copy-start.4
  48.9 20.1 %collective-permute-start.2 = (bf16[256,1664]{1,0:T(8,128)(2,1)}, bf16[256,1664]{1,0:T(8,128)(2,1)}, u32[]{:S(2)}, u32[]{:S(2)}) collective-permute-start(bf16[256,1664]{1,0:T(8,128)(2,1)} %bitcast.4.block_ref.refs_0_), channel_id=1, source_target_pairs={{0,33},{1,34},{2,35},{3,36},{4,37},{5,38},{6,39},{7,32},{8,41},{9,... | collective-permute-start | bytes 2555912 | tf_op jit(solution)/shard_map/ppermute | solution.py:233
  50.8 21.5 %collective-permute-start.3 = (bf16[256,1664]{1,0:T(8,128)(2,1)}, bf16[256,1664]{1,0:T(8,128)(2,1)}, u32[]{:S(2)}, u32[]{:S(2)}) collective-permute-start(bf16[256,1664]{1,0:T(8,128)(2,1)} %bitcast.4.block_ref.refs_0_), channel_id=1, source_target_pairs={{0,8},{1,9},{2,10},{3,11},{4,12},{5,13},{6,14},{7,15},{8,16},{9,17... | collective-permute-start | bytes 2555912 | tf_op jit(solution)/shard_map/ppermute | solution.py:233
  54.9 22.3 %collective-permute-start.4 = (bf16[256,1664]{1,0:T(8,128)(2,1)}, bf16[256,1664]{1,0:T(8,128)(2,1)}, u32[]{:S(2)}, u32[]{:S(2)}) collective-permute-start(bf16[256,1664]{1,0:T(8,128)(2,1)} %bitcast.4.block_ref.refs_0_), channel_id=1, source_target_pairs={{0,32},{1,33},{2,34},{3,35},{4,36},{5,37},{6,38},{7,39},{8,40},{9,... | collective-permute-start | bytes 2555912 | tf_op jit(solution)/shard_map/ppermute | solution.py:233
  62.3 14.9 %collective-permute-start.5 = (bf16[256,1664]{1,0:T(8,128)(2,1)}, bf16[256,1664]{1,0:T(8,128)(2,1)}, u32[]{:S(2)}, u32[]{:S(2)}) collective-permute-start(bf16[256,1664]{1,0:T(8,128)(2,1)} %bitcast.4.block_ref.refs_0_), channel_id=1, source_target_pairs={{0,1},{1,2},{2,3},{3,4},{4,5},{5,6},{6,7},{7,0},{8,9},{9,10},{10,1... | collective-permute-start | bytes 2555912 | tf_op jit(solution)/shard_map/ppermute | solution.py:233
  64.2 20.7 %collective-permute-start.6 = (bf16[256,1664]{1,0:T(8,128)(2,1)}, bf16[256,1664]{1,0:T(8,128)(2,1)}, u32[]{:S(2)}, u32[]{:S(2)}) collective-permute-start(bf16[256,1664]{1,0:T(8,128)(2,1)} %bitcast.4.block_ref.refs_0_), channel_id=1, source_target_pairs={{0,416},{1,417},{2,418},{3,419},{4,420},{5,421},{6,422},{7,423},{8... | collective-permute-start | bytes 2555912 | tf_op jit(solution)/shard_map/ppermute | solution.py:233
  67.8 1.2 %copy-start.1 = (f32[256,1664]{1,0:T(8,128)}, f32[256,1664]{1,0:T(8,128)S(1)}, u32[]{:S(2)}) copy-start(f32[256,1664]{1,0:T(8,128)S(1)} %shard_map.64.refs_6_) | copy-start | bytes 5111812
  69.0 23.2 %collective-permute-start.7 = (bf16[256,1664]{1,0:T(8,128)(2,1)}, bf16[256,1664]{1,0:T(8,128)(2,1)}, u32[]{:S(2)}, u32[]{:S(2)}) collective-permute-start(bf16[256,1664]{1,0:T(8,128)(2,1)} %bitcast.4.block_ref.refs_0_), channel_id=1, source_target_pairs={{0,7},{1,0},{2,1},{3,2},{4,3},{5,4},{6,5},{7,6},{8,15},{9,8},{10,9... | collective-permute-start | bytes 2555912 | tf_op jit(solution)/shard_map/ppermute | solution.py:236
  72.4 19.8 %collective-permute-start.8 = (bf16[256,1664]{1,0:T(8,128)(2,1)}, bf16[256,1664]{1,0:T(8,128)(2,1)}, u32[]{:S(2)}, u32[]{:S(2)}) collective-permute-start(bf16[256,1664]{1,0:T(8,128)(2,1)} %bitcast.4.block_ref.refs_0_), channel_id=1, source_target_pairs={{0,24},{1,25},{2,26},{3,27},{4,28},{5,29},{6,30},{7,31},{8,0},{9,1... | collective-permute-start | bytes 2555912 | tf_op jit(solution)/shard_map/ppermute | solution.py:236
  84.9 1.5 %copy-start.2 = (f32[256,1664]{1,0:T(8,128)S(1)}, f32[256,1664]{1,0:T(8,128)}, u32[]{:S(2)}) copy-start(f32[256,1664]{1,0:T(8,128)} %copy-done.1) | copy-start | bytes 5111812
  86.3 5.9 %copy-start.5 = (bf16[256,1664]{1,0:T(8,128)(2,1)S(1)}, bf16[256,1664]{1,0:T(8,128)(2,1)}, u32[]{:S(2)}) copy-start(bf16[256,1664]{1,0:T(8,128)(2,1)} %copy-done.4) | copy-start | bytes 2555908
  92.2 4.7 %copy-start.3 = (bf16[256,1664]{1,0:T(8,128)(2,1)S(1)}, bf16[256,1664]{1,0:T(8,128)(2,1)}, u32[]{:S(2)}) copy-start(bf16[256,1664]{1,0:T(8,128)(2,1)} %get-tuple-element.14.stream_ref) | copy-start | bytes 2555908
  94.9 4.6 %collective-permute-start.9 = (bf16[256,1664]{1,0:T(8,128)(2,1)S(1)}, bf16[256,1664]{1,0:T(8,128)(2,1)S(1)}, u32[]{:S(2)}, u32[]{:S(2)}) collective-permute-start(bf16[256,1664]{1,0:T(8,128)(2,1)S(1)} %shard_map.67), channel_id=1, source_target_pairs={{0,64},{1,65},{2,66},{3,67},{4,68},{5,69},{6,70},{7,71},{8,72},{9,... | collective-permute-start | bytes 2555912 | tf_op jit(solution)/shard_map/ppermute | solution.py:240

commit v5 on v4

--- a/solution.py
+++ b/solution.py
@@ -243,7 +243,7 @@
 
 
 AHEAD = 5
-SOON = 6
+SOON = 5
 
 
 def solution(mesh):

time: 102 us -> 104 us (1.020)
  the two profiles are of different devices: /device:TPU:1 before, /device:TPU:25 now
where the time goes in v5:
time: 104 us; the launch traced here: 103 us
  starting transfers between devices  51.5 us (50%)
  waiting for transfers between devices  21.6 us (21%)
  Pallas kernels  14.3 us (14%)
  local copies, waits for them, and re-layouts  7.82 us (8%)
  matrix products  3.25 us (3%)
  blocking collectives  2.5 us (2%)
  other arithmetic  1.76 us (2%)
    all_to_all x1, starting transfers between devices, body(): lax.all_to_all(for_each, 'd', 0, 0, axis_index_groups=GROUPS, tiled=True)  18 us
    ppermute x5, starting transfers between devices, body(): lax.ppermute(block, 'd', moves(*step))  15 us
    all_to_all x1, waiting for transfers between devices, body(): lax.all_to_all(for_each, 'd', 0, 0, axis_index_groups=GROUPS, tiled=True)  13.9 us
    ppermute x1, starting transfers between devices, body(): came = lax.ppermute(other, 'd', OTHER_CORE)  8.5 us
    pallas_call x2, Pallas kernels, late(): pl.pallas_call(functools.partial(late_kernel, slice(half * TOK, (half + 1...  6.4 us
    ppermute x5, waiting for transfers between devices, body(): lax.ppermute(block, 'd', moves(*step))  5.99 us
    ppermute x2, starting transfers between devices, body(): blocks += [lax.ppermute(block, 'd', moves(*step)) for step in STEPS[AHEAD:]]  5.27 us
    pallas_call x1, Pallas kernels, early(): pl.pallas_call(functools.partial(early_kernel, n), in_specs=[SMEM_SPEC, V...  5.11 us
  transfers between devices with their start and end apart: 11, of which 5 were waited for; matrix products, arithmetic and copies ran while one was open for 8% of the time, Pallas kernels for 10%

profile of v5, /device:TPU:25, one launch (start us, length us, event | category | flops | bytes accessed | tf_op | source)
XLA Modules:
  0.0 103.2 jit_solution(10035535318262580086)
XLA Ops:
  0.0 0.0 copy-start
  0.0 2.5 %all-gather.1 = bf16[2,4,3200]{2,1,0:T(4,128)(2,1)S(1)} all-gather(bf16[1,4,3200]{2,1,0:T(4,128)(2,1)} %bitcast.19), channel_id=2, replica_groups={{0,64},{1,65},{2,66},{3,67},{4,68},{5,69},{6,70},{7,71},{8,72},{9,73},{..., dimensions={0}, use_global_device_ids=true | all-gather | bytes 76800 | tf_op jit(solution)/shard_map/all_gather | solution.py:216
  2.5 1.0 broadcast_in_dim.8
  3.5 18.0 %all-to-all-start = ((bf16[32,8,1664]{2,1,0:T(8,128)(2,1)}), bf16[32,8,1664]{2,1,0:T(8,128)(2,1)}, u32[]{:S(2)}, u32[]{:S(2)}) async-start(bf16[32,8,1664]{2,1,0:T(8,128)(2,1)} %broadcast_in_dim.8), calls=%async_computation | async-start | bytes 1703936 | tf_op jit(solution)/shard_map/all_to_all | solution.py:219
  21.5 0.0 copy-done
  21.5 3.3 %fusion.4 = bf16[2048,256]{1,0:T(8,128)(2,1)S(1)} fusion(bf16[256,2048]{1,0:T(8,128)(2,1)S(1)} %copy-done, s32[2048]{0:T(1024)} %constant.141), kind=kOutput, calls=%fused_computation.4 | convolution fusion | flops 2156396544 | bytes 2105344 | tf_op jit(solution)/shard_map/dot_general | solution.py:222
  24.8 0.5 copy.8
  25.3 0.0 copy-start.6
  25.3 2.8 %collective-permute-start = (bf16[8,256,256]{2,1,0:T(8,128)(2,1)S(1)}, bf16[8,256,256]{2,1,0:T(8,128)(2,1)}, u32[]{:S(2)}, u32[]{:S(2)}) collective-permute-start(bf16[8,256,256]{2,1,0:T(8,128)(2,1)S(1)} %bitcast.16), channel_id=1, source_target_pairs={{0,64},{1,65},{2,66},{3,67},{4,68},{5,69},{6,70},{7,71},{8,72},{9,... | collective-permute-start | bytes 3145736 | tf_op jit(solution)/shard_map/ppermute | solution.py:224
  28.2 2.4 %constant_dynamic-slice_fusion = (bf16[256,1664]{1,0:T(8,128)(2,1)S(1)}, bf16[256,1664]{1,0:T(8,128)(2,1)}) fusion(bf16[256,3200]{1,0:T(8,128)(2,1)} %param.6, s32[]{:T(128)S(6)} %select_n.86, s32[]{:T(128)S(6)} %select_n.85), kind=kLoop, calls=%fused_computation.6 | loop fusion | bytes 3407880 | tf_op jit(solution)/shard_map/dynamic_slice | solution.py:226
  30.6 1.9 %collective-permute-start.1 = (bf16[256,1664]{1,0:T(8,128)(2,1)S(1)}, bf16[256,1664]{1,0:T(8,128)(2,1)S(1)}, u32[]{:S(2)}, u32[]{:S(2)}) collective-permute-start(bf16[256,1664]{1,0:T(8,128)(2,1)S(1)} %get-tuple-element.17), channel_id=1, source_target_pairs={{0,64},{1,65},{2,66},{3,67},{4,68},{5,69},{6,70},{7,71},{8,72},{9,... | collective-permute-start | bytes 2555912 | tf_op jit(solution)/shard_map/ppermute | solution.py:226
  32.5 0.0 copy-done.6
  32.5 0.0 collective-permute-done
  32.5 1.7 %pad_maximum_fusion.heads_ref = bf16[8,512,256]{2,1,0:T(8,128)(2,1)S(1)} fusion(bf16[8,256,256]{2,1,0:T(8,128)(2,1)} %bitcast.17, bf16[8,256,256]{2,1,0:T(8,128)(2,1)} %collective-permute-done), kind=kLoop, calls=%fused_computation.5 | loop fusion | flops 4194304 | bytes 4194304 | tf_op jit(solution)/shard_map/concatenate | solution.py:229
  34.2 0.0 copy-start.7
  34.2 0.0 copy-start.8
  34.3 0.6 collective-permute-done.1.stream_ref
  34.9 0.0 copy-start.4
  34.9 0.9 copy-done.4
  35.8 13.9 %all-to-all-done = bf16[32,8,1664]{2,1,0:T(8,128)(2,1)} async-done(((bf16[32,8,1664]{2,1,0:T(8,128)(2,1)}), bf16[32,8,1664]{2,1,0:T(8,128)(2,1)}, u32[]{:S(2)}, u32[]{:S(2)}) %all-to-all-start) | async-done | bytes 852000 | tf_op jit(solution)/shard_map/all_to_all | solution.py:219
  49.6 1.9 %collective-permute-start.2 = (bf16[256,1664]{1,0:T(8,128)(2,1)}, bf16[256,1664]{1,0:T(8,128)(2,1)}, u32[]{:S(2)}, u32[]{:S(2)}) collective-permute-start(bf16[256,1664]{1,0:T(8,128)(2,1)} %bitcast.5.block_ref.refs_0_), channel_id=1, source_target_pairs={{0,33},{1,34},{2,35},{3,36},{4,37},{5,38},{6,39},{7,32},{8,41},{9,... | collective-permute-start | bytes 2555912 | tf_op jit(solution)/shard_map/ppermute | solution.py:233
  51.6 4.6 %collective-permute-start.3 = (bf16[256,1664]{1,0:T(8,128)(2,1)}, bf16[256,1664]{1,0:T(8,128)(2,1)}, u32[]{:S(2)}, u32[]{:S(2)}) collective-permute-start(bf16[256,1664]{1,0:T(8,128)(2,1)} %bitcast.5.block_ref.refs_0_), channel_id=1, source_target_pairs={{0,8},{1,9},{2,10},{3,11},{4,12},{5,13},{6,14},{7,15},{8,16},{9,17... | collective-permute-start | bytes 2555912 | tf_op jit(solution)/shard_map/ppermute | solution.py:233
  56.2 1.9 %collective-permute-start.4 = (bf16[256,1664]{1,0:T(8,128)(2,1)}, bf16[256,1664]{1,0:T(8,128)(2,1)}, u32[]{:S(2)}, u32[]{:S(2)}) collective-permute-start(bf16[256,1664]{1,0:T(8,128)(2,1)} %bitcast.5.block_ref.refs_0_), channel_id=1, source_target_pairs={{0,32},{1,33},{2,34},{3,35},{4,36},{5,37},{6,38},{7,39},{8,40},{9,... | collective-permute-start | bytes 2555912 | tf_op jit(solution)/shard_map/ppermute | solution.py:233
  58.1 1.9 %collective-permute-start.5 = (bf16[256,1664]{1,0:T(8,128)(2,1)}, bf16[256,1664]{1,0:T(8,128)(2,1)}, u32[]{:S(2)}, u32[]{:S(2)}) collective-permute-start(bf16[256,1664]{1,0:T(8,128)(2,1)} %bitcast.5.block_ref.refs_0_), channel_id=1, source_target_pairs={{0,1},{1,2},{2,3},{3,4},{4,5},{5,6},{6,7},{7,0},{8,9},{9,10},{10,1... | collective-permute-start | bytes 2555912 | tf_op jit(solution)/shard_map/ppermute | solution.py:233
  60.1 1.6 %shard_map.64.refs_5_ = f32[256,1664]{1,0:T(8,128)S(1)} custom-call(s32[1]{0:T(128)} %bitcast.9.rank_ref, bf16[8,512,256]{2,1,0:T(8,128)(2,1)S(1)} %pad_maximum_fusion.heads_ref, bf16[256,1664]{1,0:T(8,128)(2,1)} %bitcast.5.block_ref.refs_0_), custom_call_target="tpu_custom_call" | custom-call | flops 218103808 | bytes 851968 | tf_op jit(solution)/shard_map/pallas_call | solution.py:139
  61.7 0.0 copy-start.1
  61.7 1.2 %copy-done.1 = f32[256,1664]{1,0:T(8,128)} copy-done((f32[256,1664]{1,0:T(8,128)}, f32[256,1664]{1,0:T(8,128)S(1)}, u32[]{:S(2)}) %copy-start.1) | copy-done | bytes 1703960
  62.9 3.4 %collective-permute-start.7 = (bf16[256,1664]{1,0:T(8,128)(2,1)}, bf16[256,1664]{1,0:T(8,128)(2,1)}, u32[]{:S(2)}, u32[]{:S(2)}) collective-permute-start(bf16[256,1664]{1,0:T(8,128)(2,1)} %bitcast.5.block_ref.refs_0_), channel_id=1, source_target_pairs={{0,7},{1,0},{2,1},{3,2},{4,3},{5,4},{6,5},{7,6},{8,15},{9,8},{10,9... | collective-permute-start | bytes 2555912 | tf_op jit(solution)/shard_map/ppermute | solution.py:236
  66.3 0.0 collective-permute-done.2.refs_1_
  66.3 1.9 %collective-permute-start.8 = (bf16[256,1664]{1,0:T(8,128)(2,1)}, bf16[256,1664]{1,0:T(8,128)(2,1)}, u32[]{:S(2)}, u32[]{:S(2)}) collective-permute-start(bf16[256,1664]{1,0:T(8,128)(2,1)} %bitcast.5.block_ref.refs_0_), channel_id=1, source_target_pairs={{0,24},{1,25},{2,26},{3,27},{4,28},{5,29},{6,30},{7,31},{8,0},{9,1... | collective-permute-start | bytes 2555912 | tf_op jit(solution)/shard_map/ppermute | solution.py:236
  68.2 0.0 collective-permute-done.3.refs_2_
  68.3 4.6 %collective-permute-start.6 = (bf16[256,1664]{1,0:T(8,128)(2,1)}, bf16[256,1664]{1,0:T(8,128)(2,1)}, u32[]{:S(2)}, u32[]{:S(2)}) collective-permute-start(bf16[256,1664]{1,0:T(8,128)(2,1)} %bitcast.5.block_ref.refs_0_), channel_id=1, source_target_pairs={{0,416},{1,417},{2,418},{3,419},{4,420},{5,421},{6,422},{7,423},{8... | collective-permute-start | bytes 2555912 | tf_op jit(solution)/shard_map/ppermute | solution.py:233
  73.0 0.0 copy-done.7
  73.0 0.1 dynamic_slice.18
  73.1 0.0 copy-done.8
  73.1 0.1 dynamic_slice.19
  73.2 0.1 stack.38.rank_ref
  73.2 0.1 pad_add_fusion.rank_ref
  73.3 0.8 collective-permute-done.4.refs_3_
  74.1 5.2 %collective-permute-done.5.refs_4_ = bf16[256,1664]{1,0:T(8,128)(2,1)} collective-permute-done((bf16[256,1664]{1,0:T(8,128)(2,1)}, bf16[256,1664]{1,0:T(8,128)(2,1)}, u32[]{:S(2)}, u32[]{:S(2)}) %collective-permute-start.5) | collective-permute-done | bytes 852000 | tf_op jit(solution)/shard_map/ppermute | solution.py:233
  79.3 0.0 copy-start.2
  79.3 1.5 %copy-done.2 = f32[256,1664]{1,0:T(8,128)S(1)} copy-done((f32[256,1664]{1,0:T(8,128)S(1)}, f32[256,1664]{1,0:T(8,128)}, u32[]{:S(2)}) %copy-start.2) | copy-done | bytes 1703960
  80.8 0.0 copy-start.5
  80.8 5.1 %shard_map.65.so_far_ref = f32[512,1664]{1,0:T(8,128)S(1)} custom-call(s32[5]{0:T(128)S(1)} %stack.38.rank_ref, bf16[8,512,256]{2,1,0:T(8,128)(2,1)S(1)} %pad_maximum_fusion.heads_ref, bf16[256,1664]{1,0:T(8,128)(2,1)} %bitcast.5.block_ref.refs_0_, bf16[256,1664]{1,0:T(8,128)(2,1)} %collective-permute-done.2.refs_1_, ...), custom_call_target="tpu_custom_call" | custom-call | flops 2181038080 | bytes 4259840 | tf_op jit(solution)/shard_map/pallas_call | solution.py:152
  85.9 0.0 copy-start.3
  85.9 1.1 %collective-permute-done.7.refs_1_ = bf16[256,1664]{1,0:T(8,128)(2,1)} collective-permute-done((bf16[256,1664]{1,0:T(8,128)(2,1)}, bf16[256,1664]{1,0:T(8,128)(2,1)}, u32[]{:S(2)}, u32[]{:S(2)}) %collective-permute-start.7) | collective-permute-done | bytes 852000 | tf_op jit(solution)/shard_map/ppermute | solution.py:236
  87.0 0.0 collective-permute-done.8.refs_2_
  87.0 0.0 collective-permute-done.6.refs_0_
  87.0 0.0 copy-done.5
  87.0 3.2 %shard_map.67 = bf16[256,1664]{1,0:T(8,128)(2,1)S(1)} custom-call(s32[3]{0:T(128)S(1)} %pad_add_fusion.rank_ref, bf16[8,512,256]{2,1,0:T(8,128)(2,1)S(1)} %pad_maximum_fusion.heads_ref, f32[512,1664]{1,0:T(8,128)S(1)} %shard_map.65.so_far_ref, bf16[256,1664]{1,0:T(8,128)(2,1)S(1)} %copy-done.5, f32[1,1664]{1,0:T(1,128)S(1)} %reshape.20.scale_ref, ...), custom_call_target="tpu_custom_call" | custom-call | flops 654311424 | bytes 2555904 | tf_op jit(solution)/shard_map/pallas_call | solution.py:165
  90.2 8.5 %collective-permute-start.9 = (bf16[256,1664]{1,0:T(8,128)(2,1)S(1)}, bf16[256,1664]{1,0:T(8,128)(2,1)S(1)}, u32[]{:S(2)}, u32[]{:S(2)}) collective-permute-start(bf16[256,1664]{1,0:T(8,128)(2,1)S(1)} %shard_map.67), channel_id=1, source_target_pairs={{0,64},{1,65},{2,66},{3,67},{4,68},{5,69},{6,70},{7,71},{8,72},{9,... | collective-permute-start | bytes 2555912 | tf_op jit(solution)/shard_map/ppermute | solution.py:240
  98.7 0.0 copy-done.3
  98.7 3.2 %shard_map.66.own_ref = bf16[256,1664]{1,0:T(8,128)(2,1)S(1)} custom-call(s32[3]{0:T(128)S(1)} %pad_add_fusion.rank_ref, bf16[8,512,256]{2,1,0:T(8,128)(2,1)S(1)} %pad_maximum_fusion.heads_ref, f32[512,1664]{1,0:T(8,128)S(1)} %shard_map.65.so_far_ref, bf16[256,1664]{1,0:T(8,128)(2,1)S(1)} %copy-done.3, f32[1,1664]{1,0:T(1,128)S(1)} %reshape.20.scale_ref, ...), custom_call_target="tpu_custom_call" | custom-call | flops 654311424 | bytes 2555904 | tf_op jit(solution)/shard_map/pallas_call | solution.py:165
  101.9 0.0 collective-permute-done.9.other_ref
  101.9 1.3 %shard_map.68 = bf16[256,3200]{1,0:T(8,128)(2,1)} custom-call(s32[1]{0:T(128)} %bitcast.core_ref, bf16[256,1664]{1,0:T(8,128)(2,1)S(1)} %shard_map.66.own_ref, bf16[256,1664]{1,0:T(8,128)(2,1)S(1)} %collective-permute-done.9.other_ref), custom_call_target="tpu_custom_call" | custom-call | tf_op jit(solution)/shard_map/pallas_call | solution.py:190
  (4 shorter events, 0.0 us)
Async XLA Ops:
  0.0 21.5 %copy-start = (bf16[256,2048]{1,0:T(8,128)(2,1)S(1)}, bf16[256,2048]{1,0:T(8,128)(2,1)}, u32[]{:S(2)}) copy-start(bf16[256,2048]{1,0:T(8,128)(2,1)} %param.7) | copy-start | bytes 3145732
  3.5 46.1 %all-to-all-start = ((bf16[32,8,1664]{2,1,0:T(8,128)(2,1)}), bf16[32,8,1664]{2,1,0:T(8,128)(2,1)}, u32[]{:S(2)}, u32[]{:S(2)}) async-start(bf16[32,8,1664]{2,1,0:T(8,128)(2,1)} %broadcast_in_dim.8), calls=%async_computation | async-start | bytes 1703936 | tf_op jit(solution)/shard_map/all_to_all | solution.py:219
  25.3 7.2 %copy-start.6 = (bf16[256,8,256]{2,0,1:T(8,128)(2,1)}, bf16[256,8,256]{2,0,1:T(8,128)(2,1)S(1)}, u32[]{:S(2)}) copy-start(bf16[256,8,256]{2,0,1:T(8,128)(2,1)S(1)} %copy.8) | copy-start | bytes 3145732
  25.3 7.2 %collective-permute-start = (bf16[8,256,256]{2,1,0:T(8,128)(2,1)S(1)}, bf16[8,256,256]{2,1,0:T(8,128)(2,1)}, u32[]{:S(2)}, u32[]{:S(2)}) collective-permute-start(bf16[8,256,256]{2,1,0:T(8,128)(2,1)S(1)} %bitcast.16), channel_id=1, source_target_pairs={{0,64},{1,65},{2,66},{3,67},{4,68},{5,69},{6,70},{7,71},{8,72},{9,... | collective-permute-start | bytes 3145736 | tf_op jit(solution)/shard_map/ppermute | solution.py:224
  30.6 4.3 %collective-permute-start.1 = (bf16[256,1664]{1,0:T(8,128)(2,1)S(1)}, bf16[256,1664]{1,0:T(8,128)(2,1)S(1)}, u32[]{:S(2)}, u32[]{:S(2)}) collective-permute-start(bf16[256,1664]{1,0:T(8,128)(2,1)S(1)} %get-tuple-element.17), channel_id=1, source_target_pairs={{0,64},{1,65},{2,66},{3,67},{4,68},{5,69},{6,70},{7,71},{8,72},{9,... | collective-permute-start | bytes 2555912 | tf_op jit(solution)/shard_map/ppermute | solution.py:226
  34.2 38.7 %copy-start.7 = (f32[3200]{0:T(1024)S(1)}, f32[3200]{0:T(1024)}, u32[]{:S(2)}) copy-start(f32[3200]{0:T(1024)} %param.10) | copy-start | bytes 38404
  34.2 38.8 %copy-start.8 = (f32[3200]{0:T(1024)S(1)}, f32[3200]{0:T(1024)}, u32[]{:S(2)}) copy-start(f32[3200]{0:T(1024)} %param.9) | copy-start | bytes 38404
  34.9 0.9 copy-start.4
  49.6 16.7 %collective-permute-start.2 = (bf16[256,1664]{1,0:T(8,128)(2,1)}, bf16[256,1664]{1,0:T(8,128)(2,1)}, u32[]{:S(2)}, u32[]{:S(2)}) collective-permute-start(bf16[256,1664]{1,0:T(8,128)(2,1)} %bitcast.5.block_ref.refs_0_), channel_id=1, source_target_pairs={{0,33},{1,34},{2,35},{3,36},{4,37},{5,38},{6,39},{7,32},{8,41},{9,... | collective-permute-start | bytes 2555912 | tf_op jit(solution)/shard_map/ppermute | solution.py:233
  51.6 16.7 %collective-permute-start.3 = (bf16[256,1664]{1,0:T(8,128)(2,1)}, bf16[256,1664]{1,0:T(8,128)(2,1)}, u32[]{:S(2)}, u32[]{:S(2)}) collective-permute-start(bf16[256,1664]{1,0:T(8,128)(2,1)} %bitcast.5.block_ref.refs_0_), channel_id=1, source_target_pairs={{0,8},{1,9},{2,10},{3,11},{4,12},{5,13},{6,14},{7,15},{8,16},{9,17... | collective-permute-start | bytes 2555912 | tf_op jit(solution)/shard_map/ppermute | solution.py:233
  56.2 17.9 %collective-permute-start.4 = (bf16[256,1664]{1,0:T(8,128)(2,1)}, bf16[256,1664]{1,0:T(8,128)(2,1)}, u32[]{:S(2)}, u32[]{:S(2)}) collective-permute-start(bf16[256,1664]{1,0:T(8,128)(2,1)} %bitcast.5.block_ref.refs_0_), channel_id=1, source_target_pairs={{0,32},{1,33},{2,34},{3,35},{4,36},{5,37},{6,38},{7,39},{8,40},{9,... | collective-permute-start | bytes 2555912 | tf_op jit(solution)/shard_map/ppermute | solution.py:233
  58.1 21.2 %collective-permute-start.5 = (bf16[256,1664]{1,0:T(8,128)(2,1)}, bf16[256,1664]{1,0:T(8,128)(2,1)}, u32[]{:S(2)}, u32[]{:S(2)}) collective-permute-start(bf16[256,1664]{1,0:T(8,128)(2,1)} %bitcast.5.block_ref.refs_0_), channel_id=1, source_target_pairs={{0,1},{1,2},{2,3},{3,4},{4,5},{5,6},{6,7},{7,0},{8,9},{9,10},{10,1... | collective-permute-start | bytes 2555912 | tf_op jit(solution)/shard_map/ppermute | solution.py:233
  61.7 1.2 %copy-start.1 = (f32[256,1664]{1,0:T(8,128)}, f32[256,1664]{1,0:T(8,128)S(1)}, u32[]{:S(2)}) copy-start(f32[256,1664]{1,0:T(8,128)S(1)} %shard_map.64.refs_5_) | copy-start | bytes 5111812
  62.9 24.0 %collective-permute-start.7 = (bf16[256,1664]{1,0:T(8,128)(2,1)}, bf16[256,1664]{1,0:T(8,128)(2,1)}, u32[]{:S(2)}, u32[]{:S(2)}) collective-permute-start(bf16[256,1664]{1,0:T(8,128)(2,1)} %bitcast.5.block_ref.refs_0_), channel_id=1, source_target_pairs={{0,7},{1,0},{2,1},{3,2},{4,3},{5,4},{6,5},{7,6},{8,15},{9,8},{10,9... | collective-permute-start | bytes 2555912 | tf_op jit(solution)/shard_map/ppermute | solution.py:236
  66.3 20.7 %collective-permute-start.8 = (bf16[256,1664]{1,0:T(8,128)(2,1)}, bf16[256,1664]{1,0:T(8,128)(2,1)}, u32[]{:S(2)}, u32[]{:S(2)}) collective-permute-start(bf16[256,1664]{1,0:T(8,128)(2,1)} %bitcast.5.block_ref.refs_0_), channel_id=1, source_target_pairs={{0,24},{1,25},{2,26},{3,27},{4,28},{5,29},{6,30},{7,31},{8,0},{9,1... | collective-permute-start | bytes 2555912 | tf_op jit(solution)/shard_map/ppermute | solution.py:236
  68.3 18.7 %collective-permute-start.6 = (bf16[256,1664]{1,0:T(8,128)(2,1)}, bf16[256,1664]{1,0:T(8,128)(2,1)}, u32[]{:S(2)}, u32[]{:S(2)}) collective-permute-start(bf16[256,1664]{1,0:T(8,128)(2,1)} %bitcast.5.block_ref.refs_0_), channel_id=1, source_target_pairs={{0,416},{1,417},{2,418},{3,419},{4,420},{5,421},{6,422},{7,423},{8... | collective-permute-start | bytes 2555912 | tf_op jit(solution)/shard_map/ppermute | solution.py:233
  79.3 1.5 %copy-start.2 = (f32[256,1664]{1,0:T(8,128)S(1)}, f32[256,1664]{1,0:T(8,128)}, u32[]{:S(2)}) copy-start(f32[256,1664]{1,0:T(8,128)} %copy-done.1) | copy-start | bytes 5111812
  80.8 6.2 %copy-start.5 = (bf16[256,1664]{1,0:T(8,128)(2,1)S(1)}, bf16[256,1664]{1,0:T(8,128)(2,1)}, u32[]{:S(2)}) copy-start(bf16[256,1664]{1,0:T(8,128)(2,1)} %copy-done.4) | copy-start | bytes 2555908
  85.9 12.8 %copy-start.3 = (bf16[256,1664]{1,0:T(8,128)(2,1)S(1)}, bf16[256,1664]{1,0:T(8,128)(2,1)}, u32[]{:S(2)}) copy-start(bf16[256,1664]{1,0:T(8,128)(2,1)} %get-tuple-element.14.stream_ref) | copy-start | bytes 2555908
  90.2 11.7 %collective-permute-start.9 = (bf16[256,1664]{1,0:T(8,128)(2,1)S(1)}, bf16[256,1664]{1,0:T(8,128)(2,1)S(1)}, u32[]{:S(2)}, u32[]{:S(2)}) collective-permute-start(bf16[256,1664]{1,0:T(8,128)(2,1)S(1)} %shard_map.67), channel_id=1, source_target_pairs={{0,64},{1,65},{2,66},{3,67},{4,68},{5,69},{6,70},{7,71},{8,72},{9,... | collective-permute-start | bytes 2555912 | tf_op jit(solution)/shard_map/ppermute | solution.py:240
